TPU v7x, 128 devices: a whole 4x4x4 slice. The times are simulated.
128 devices in a mesh: role: 4 (over x), ctx: 32 (over z, y, core).
Axes of the slice: x: 4, y: 4, z: 4, core: 2. Of those that a mesh axis runs over, the one named last changes fastest.
Arguments:
- prefill_hidden: bfloat16 [131072, 7168], P(('role', 'ctx')), may hold values from -6 to 6
- kv_down: bfloat16 [7168, 576], P('ctx'), may hold values from -0.0625 to 0.0625
- kv_gain: float32 [512], replicated, may hold values from 0.5 to 1.5
- q_nope: bfloat16 [8, 2, 128, 128], P('role', None, 'ctx'), may hold values from -8 to 8
- q_rope: bfloat16 [8, 2, 128, 64], P('role', None, 'ctx'), may hold values from -8 to 8
- key_up: bfloat16 [128, 128, 512], P('ctx'), may hold values from -0.5 to 0.5
- value_up: bfloat16 [128, 512, 128], P('ctx'), may hold values from -0.25 to 0.25
- latent_cache: bfloat16 [8, 32768, 576], P('role', 'ctx'), may hold values from -8 to 8
- cache_len: int32 [8], replicated, may hold values from 4096 to 32768
- page_list: int32 [32768, 1], replicated, may hold values from 0 to 255; in each aligned block of 256 rows (0 to 255, 256 to 511, ...) at most 2 rows name the same one
Outputs:
- attn_out: bfloat16 [8, 2, 128, 128], P('role', None, 'ctx')
Inputs may be any that keep to these rules, and one draw needn't show every extreme that they name: `page_list`: aligned blocks of 256 pages are one device's pages; within one block no destination is named by more than 2 pages.
All inputs are finite; a program needn't handle non-finite values.
Results may differ from a plain program's by a relative error of at most 0.013.
Values may be sent and summed in bfloat16 or wider, within the bound.
A program may use at most 192 MiB of HBM per device.

v0:
```python
import math

import jax
import jax.numpy as jnp
from jax import lax
from jax.sharding import PartitionSpec as P

LATENT = 512
PAGE = 4


def joined(value, axis, join):
    pieces = jax.tree.map(lambda part: lax.all_gather(part, axis), value)
    head = jax.tree.map(lambda part: part[0], pieces)
    tail = jax.tree.map(lambda part: part[1:], pieces)
    total, _ = lax.scan(lambda total, piece: (join(total, piece), None), head, tail)
    return total


def combine_parts(first, second):
    first_best, first_total, first_sum = first
    second_best, second_total, second_sum = second
    best = jnp.maximum(first_best, second_best)
    first_factor = jnp.exp(first_best - best)
    second_factor = jnp.exp(second_best - best)
    return (
        best,
        first_total * first_factor + second_total * second_factor,
        first_sum * first_factor[..., None] + second_sum * second_factor[..., None],
    )


def masked_part(queries, keys, live, scale):
    scores = jnp.dot(queries, keys.T, preferred_element_type=jnp.float32) * scale
    return (scores, live)


def local(
    prefill_hidden,
    kv_down,
    kv_gain,
    q_nope,
    q_rope,
    key_up,
    value_up,
    latent_cache,
    cache_len,
    page_list,
):
    count_ctx = lax.axis_size("ctx")
    count_role = lax.axis_size("role")
    ctx_index = lax.axis_index("ctx")
    role_index = lax.axis_index("role")
    my_device = role_index * count_ctx + ctx_index
    devices = count_role * count_ctx
    pref_rows = prefill_hidden.shape[0]
    req_grp = q_nope.shape[0]
    steps = q_nope.shape[1]
    width = kv_down.shape[1]
    heads_dev = q_nope.shape[2]
    heads_all = heads_dev * count_ctx
    slot_dev = latent_cache.shape[1]
    pages_dev = pref_rows // PAGE
    bin_count = devices * req_grp
    most_pages = max(1, 2 * pages_dev // bin_count)
    scale = 1.0 / math.sqrt(q_nope.shape[3] + q_rope.shape[3])
    low = jnp.float32(-1e30)
    projected = jnp.dot(
        prefill_hidden,
        lax.all_gather(kv_down, "ctx", axis=0, tiled=True),
        preferred_element_type=jnp.float32,
    )
    latent_part = projected[:, :LATENT]
    inverse = lax.rsqrt(jnp.mean(latent_part * latent_part, axis=-1, keepdims=True) + 1e-06)
    new_rows = jnp.concatenate(
        [latent_part * inverse * kv_gain, projected[:, LATENT:]], axis=-1
    ).astype(jnp.bfloat16)
    all_bins = page_list[:, 0]
    own_bins = lax.dynamic_slice_in_dim(all_bins, my_device * pages_dev, pages_dev)
    page_ids = jnp.arange(pages_dev, dtype=jnp.int32)
    earlier = (own_bins[:, None] == own_bins[None, :]) & (page_ids[None, :] < page_ids[:, None])
    page_rank = jnp.sum(earlier.astype(jnp.int32), axis=1)
    slot_ids = own_bins * most_pages + page_rank
    selector = (
        slot_ids[None, :] == jnp.arange(bin_count * most_pages, dtype=jnp.int32)[:, None]
    ).astype(jnp.bfloat16)
    packed = jnp.dot(
        selector, new_rows.reshape(pages_dev, PAGE * width), preferred_element_type=jnp.float32
    ).astype(jnp.bfloat16)
    packed = packed.reshape(devices, req_grp, most_pages * PAGE, width)
    arrived = lax.all_to_all(packed, ("role", "ctx"), split_axis=0, concat_axis=0, tiled=True)
    targets = my_device * req_grp + jnp.arange(req_grp, dtype=jnp.int32)
    sent_counts = jnp.sum(
        (all_bins.reshape(devices, pages_dev)[:, :, None] == targets[None, None, :]).astype(
            jnp.int32
        ),
        axis=1,
    )
    slot_page = jnp.arange(most_pages * PAGE, dtype=jnp.int32) // PAGE
    arrived_live = slot_page[None, None, :] < sent_counts[:, :, None]
    absorbed = jnp.einsum(
        "rthn,hnc->rthc", q_nope, key_up, preferred_element_type=jnp.float32
    ).astype(jnp.bfloat16)
    query_part = jnp.concatenate([absorbed, q_rope], axis=-1)
    full_query = lax.all_gather(query_part, "ctx", axis=2, tiled=True)
    positions = ctx_index * slot_dev + jnp.arange(slot_dev, dtype=jnp.int32)
    group_lengths = lax.dynamic_slice_in_dim(cache_len, role_index * req_grp, req_grp)
    best_list = []
    total_list = []
    summed_list = []
    for request_idx in range(req_grp):
        queries = full_query[request_idx].reshape(steps * heads_all, width)
        cache_rows = latent_cache[request_idx]
        fresh_rows = arrived[:, request_idx].reshape(devices * most_pages * PAGE, width)
        fresh_live = arrived_live[:, request_idx].reshape(devices * most_pages * PAGE)
        parts = [
            masked_part(
                queries, cache_rows, (positions < group_lengths[request_idx])[None, :], scale
            ),
            masked_part(queries, fresh_rows, fresh_live[None, :], scale),
        ]
        best = jnp.max(jnp.where(parts[0][1], parts[0][0], low), axis=1)
        for scores, live in parts[1:]:
            best = jnp.maximum(best, jnp.max(jnp.where(live, scores, low), axis=1))
        total = jnp.zeros_like(best)
        summed = jnp.zeros((steps * heads_all, LATENT), jnp.float32)
        for (scores, live), key_rows in zip(parts, [cache_rows, fresh_rows]):
            weights = jnp.where(live, jnp.exp(scores - best[:, None]), 0.0)
            total = total + jnp.sum(weights, axis=1)
            summed = summed + jnp.dot(
                weights.astype(jnp.bfloat16),
                key_rows[:, :LATENT],
                preferred_element_type=jnp.float32,
            )
        best_list.append(best.reshape(steps, heads_all))
        total_list.append(total.reshape(steps, heads_all))
        summed_list.append(summed.reshape(steps, heads_all, LATENT))
    best_all = jnp.stack(best_list)
    total_all = jnp.stack(total_list)
    summed_all = jnp.stack(summed_list)
    best, total, summed = joined((best_all, total_all, summed_all), "ctx", combine_parts)
    whole_out = summed / total[..., None]
    latent_out = lax.dynamic_slice_in_dim(whole_out, ctx_index * heads_dev, heads_dev, 2).astype(
        jnp.bfloat16
    )
    return jnp.einsum(
        "rthc,hcv->rthv", latent_out, value_up, preferred_element_type=jnp.float32
    ).astype(jnp.bfloat16)


def solution(mesh):
    return jax.shard_map(
        local,
        mesh=mesh,
        in_specs=(
            P(("role", "ctx"), None),
            P("ctx", None),
            P(),
            P("role", None, "ctx", None),
            P("role", None, "ctx", None),
            P("ctx", None, None),
            P("ctx", None, None),
            P("role", "ctx", None),
            P(),
            P(),
        ),
        out_specs=P("role", None, "ctx", None),
        check_vma=False,
    )
```

profile of v0, /device:TPU:0, one launch (start us, length us, event | category | flops | bytes accessed | tf_op | source)
XLA Modules:
  0.0 360.3 jit_solution(11765035171390795674)
XLA Ops:
  6.5 0.7 all-gather.6.cloned.1.call-update
  7.3 0.5 broadcast.83
  7.8 1.8 reduce.3
  9.7 0.7 constant_dynamic-slice_fusion.1
  10.8 56.3 %all-gather.6.cloned.1.call-done = bf16[7168,576]{1,0:T(8,128)(2,1)} async-done(((bf16[224,576]{1,0:T(8,128)(2,1)}), bf16[7168,576]{1,0:T(8,128)(2,1)}) %all-gather.6.cloned.1.call-update) | async-done | bytes 8257552 | tf_op jit(solution)/shard_map/all_gather | solution.py:70
  67.0 13.4 %fusion.62 = f32[1024,576]{0,1:T(8,128)S(1)} fusion(bf16[1024,7168]{1,0:T(8,128)(2,1)} %param.12, bf16[7168,576]{1,0:T(8,128)(2,1)} %all-gather.6.cloned.1.call-done), kind=kOutput, calls=%fused_computation.108 | convolution fusion | flops 8455716864 | bytes 25296896 | tf_op jit(solution)/shard_map/dot_general | solution.py:68
  81.4 0.7 copy.35
  82.2 2.1 convert_element_type.46
  84.3 2.1 convolution_convert_fusion
  86.4 4.0 %reshape.141 = bf16[128,2,8,576]{3,2,1,0:T(8,128)(2,1)} reshape(bf16[512,2304]{1,0:T(8,128)(2,1)S(1)} %convolution_convert_fusion) | data formatting | bytes 4718592 | tf_op jit(solution)/shard_map/reshape | solution.py:90
  90.4 8.2 %all-to-all-start = ((bf16[128,2,8,576]{3,2,1,0:T(8,128)(2,1)}), bf16[128,2,8,576]{3,2,1,0:T(8,128)(2,1)S(1)}, u32[]{:S(2)}, u32[]{:S(2)}) async-start(bf16[128,2,8,576]{3,2,1,0:T(8,128)(2,1)} %reshape.141), calls=%async_computation | async-start | bytes 5242880 | tf_op jit(solution)/shard_map/all_to_all | solution.py:91
  99.2 47.9 %all_gather.24 = bf16[2,2,128,576]{3,1,0,2:T(2,128)(2,1)S(1)} all-gather(bf16[2,2,4,576]{3,1,0,2:T(2,128)(2,1)S(1)} %pad_maximum_fusion.2), channel_id=1, replica_groups=mesh['role'=4,'ctx'=32] {'ctx'}, dimensions={2}, use_global_device_ids=true | all-gather | bytes 608256 | tf_op jit(solution)/shard_map/all_gather | solution.py:105
  147.6 1.2 copy.34
  148.8 1.0 copy.36
  149.9 0.6 fusion.61
  150.5 1.3 fusion.51
  151.8 2.9 select_reduce_fusion.1
  154.6 1.6 select_reduce_fusion.3
  156.3 1.6 slice_bitcast_fusion.3
  157.9 0.7 select_reduce_fusion.2
  158.7 0.7 select_reduce_fusion
  159.4 0.9 copy-done.8
  160.3 0.7 copy-done.9
  162.2 0.7 copy-done.7
  164.3 1.1 pad_maximum_fusion.1
  165.9 1.8 fusion.14
  168.3 21.5 %all-gather.1 = f32[64,2,128]{2,1,0:T(2,128)S(1)} all-gather(f32[2,2,128]{2,1,0:T(2,128)S(1)} %pad_maximum_fusion.4), channel_id=3, replica_groups=mesh['role'=4,'ctx'=32] {'ctx'}, dimensions={0}, use_global_device_ids=true | all-gather | bytes 67584 | tf_op jit(solution)/shard_map/all_gather | solution.py:13
  189.8 24.0 %all-gather = f32[64,2,128]{2,1,0:T(2,128)S(1)} all-gather(f32[2,2,128]{2,1,0:T(2,128)S(1)} %pad_maximum_fusion.3), channel_id=2, replica_groups=mesh['role'=4,'ctx'=32] {'ctx'}, dimensions={0}, use_global_device_ids=true | all-gather | bytes 67584 | tf_op jit(solution)/shard_map/all_gather | solution.py:13
  213.8 65.4 %all-gather.8.cloned.1.call-done = f32[64,2,128,512]{3,2,1,0:T(8,128)} async-done(((f32[2,2,128,512]{3,2,1,0:T(8,128)}), f32[64,2,128,512]{3,2,1,0:T(8,128)}) %all-gather.8.cloned.1.call-update) | async-done | bytes 33554448 | tf_op jit(solution)/shard_map/all_gather | solution.py:13
  279.2 23.6 %slice.112 = f32[62,2,128,512]{3,2,1,0:T(8,128)} slice(f32[64,2,128,512]{3,2,1,0:T(8,128)} %all-gather.8.cloned.1.call-done), slice={[2:64], [0:2], [0:128], [0:512]} | slice | bytes 65011712 | tf_op jit(solution)/shard_map/slice | solution.py:15
  302.8 48.7 %while.14 = (s32[]{:T(128)}, f32[2,2,128]{2,1,0:T(2,128)S(1)}, f32[2,2,128]{2,1,0:T(2,128)S(1)}, f32[2,2,128,512]{3,2,1,0:T(8,128)S(1)}, f32[31,2,2,128]{3,2,1,0...) while((s32[]{:T(128)}, f32[2,2,128]{2,1,0:T(2,128)S(1)}, ...), condition=%wide.region_12.13_spmd, body=%wide.region_11.12_spmd.sunk | while | flops 789506 | bytes 3166309 | solution.py:16
  302.8 1.5 fusion.69
  304.3 1.5 fusion.69
  305.9 1.5 fusion.69
  307.5 1.5 fusion.69
  309.1 1.5 fusion.69
  310.6 1.5 fusion.69
  312.2 1.5 fusion.69
  313.8 1.5 fusion.69
  315.4 1.5 fusion.69
  316.9 1.5 fusion.69
  318.5 1.5 fusion.69
  320.1 1.5 fusion.69
  321.6 1.5 fusion.69
  323.2 1.5 fusion.69
  324.8 1.5 fusion.69
  326.4 1.5 fusion.69
  327.9 1.5 fusion.69
  329.5 1.5 fusion.69
  331.1 1.5 fusion.69
  332.7 1.5 fusion.69
  334.2 1.5 fusion.69
  335.8 1.5 fusion.69
  337.4 1.5 fusion.69
  339.0 1.5 fusion.69
  340.5 1.5 fusion.69
  342.1 1.5 fusion.69
  343.7 1.5 fusion.69
  345.2 1.5 fusion.69
  346.8 1.5 fusion.69
  348.4 1.5 fusion.69
  350.0 1.5 fusion.69
  351.7 0.8 copy.38
  352.8 0.6 copy.39
  (109 shorter events, 7.4 us)
Async XLA Ops:
  6.5 92.4 %copy-start = (bf16[4,128,512]{2,1,0:T(8,128)(2,1)S(1)}, bf16[4,128,512]{2,1,0:T(8,128)(2,1)}, u32[]{:S(2)}) copy-start(bf16[4,128,512]{2,1,0:T(8,128)(2,1)} %param.17) | copy-start | bytes 1572868
  6.5 60.5 %all-gather.6.cloned.1.call-start = ((), (), s32[]{:S(2)}) async-start(), calls=%async_computation.1 | async-start | bytes 9461760 | tf_op jit(solution)/shard_map/all_gather | solution.py:70
  80.4 0.7 copy-start.15
  90.4 8.3 %copy-start.14 = (bf16[2,2,4,64]{3,2,1,0:T(4,128)(2,1)S(1)}, bf16[2,2,4,64]{3,2,1,0:T(4,128)(2,1)}, u32[]{:S(2)}) copy-start(bf16[2,2,4,64]{3,2,1,0:T(4,128)(2,1)} %param.16) | copy-start | bytes 6148
  90.4 8.6 %copy-start.13 = (bf16[2,2,4,128]{3,2,1,0:T(4,128)(2,1)S(1)}, bf16[2,2,4,128]{3,2,1,0:T(4,128)(2,1)}, u32[]{:S(2)}) copy-start(bf16[2,2,4,128]{3,2,1,0:T(4,128)(2,1)} %param.15) | copy-start | bytes 12292
  90.4 67.5 %all-to-all-start = ((bf16[128,2,8,576]{3,2,1,0:T(8,128)(2,1)}), bf16[128,2,8,576]{3,2,1,0:T(8,128)(2,1)S(1)}, u32[]{:S(2)}, u32[]{:S(2)}) async-start(bf16[128,2,8,576]{3,2,1,0:T(8,128)(2,1)} %reshape.141), calls=%async_computation | async-start | bytes 5242880 | tf_op jit(solution)/shard_map/all_to_all | solution.py:91
  98.5 51.2 %copy-start.17 = (s32[8]{0:T(128)S(1)}, s32[8]{0:T(128)}, u32[]{:S(2)}) copy-start(s32[8]{0:T(128)} %param.20) | copy-start | bytes 100
  98.6 180.6 %all-gather.8.cloned.1.call-start = ((), (), s32[]{:S(2)}) async-start(), calls=%async_computation.2 | async-start | bytes 34603008 | tf_op jit(solution)/shard_map/all_gather | solution.py:13
  149.8 4.9 %copy-start.12 = (bf16[1,2,128,576]{2,1,3,0:T(2,128)(2,1)S(1)}, bf16[1,2,128,576]{2,1,3,0:T(2,128)(2,1)}, u32[]{:S(2)}) copy-start(bf16[1,2,128,576]{2,1,3,0:T(2,128)(2,1)} %copy.34) | copy-start | bytes 884740
  149.8 4.8 %copy-start.6 = (bf16[2,1024,576]{1,2,0:T(8,128)(2,1)S(1)}, bf16[2,1024,576]{1,2,0:T(8,128)(2,1)}, u32[]{:S(2)}) copy-start(bf16[2,1024,576]{1,2,0:T(8,128)(2,1)} %param.19) | copy-start | bytes 7077892
  158.6 5.2 %copy-start.4 = (f32[256,1024]{1,0:T(8,128)}, f32[256,1024]{1,0:T(8,128)S(1)}, u32[]{:S(2)}) copy-start(f32[256,1024]{1,0:T(8,128)S(1)} %get-tuple-element.84) | copy-start | bytes 3145732
  158.6 1.7 copy-start.8
  158.6 2.3 copy-start.9
  159.4 2.3 copy-start.2
  161.7 1.3 copy-start.7
  161.7 1.6 copy-start.11
  164.3 1.6 copy-start.5
  165.4 2.4 copy-start.3
  165.4 2.4 copy-start.10
  279.2 23.6 %slice-start = ((f32[64,2,128,512]{3,2,1,0:T(8,128)}), f32[2,2,128,512]{3,2,1,0:T(8,128)S(1)}, s32[]{:S(2)}) async-start(f32[64,2,128,512]{3,2,1,0:T(8,128)} %all-gather.8.cloned.1.call-done), calls=%async_computation.3 | async-start | bytes 2097152 | tf_op jit(solution)/shard_map/slice | solution.py:14
  351.5 1.0 copy-start.16
  351.5 1.9 copy-start.1
Sparse Core Ops, SparseCore 0:
  9.6 57.3 all-gather.5
  165.5 113.5 all-gather.7
where the time goes:
time: 363 us; the launch traced here: 360 us
  waiting for transfers between devices  122 us (34%)
  blocking collectives  93.4 us (26%)
  other arithmetic  55.6 us (15%)
  local copies, waits for them, and re-layouts  42.4 us (12%)
  matrix products  23.8 us (7%)
  between operations  13.8 us (4%)
  starting transfers between devices  8.21 us (2%)
    all_gather x1, waiting for transfers between devices, joined(): pieces = jax.tree.map(lambda part: lax.all_gather(part, axis), value)  65.4 us
    all_gather x1, waiting for transfers between devices, local(): lax.all_gather(kv_down, 'ctx', axis=0, tiled=True)  56.3 us
    all_gather x1, blocking collectives, local(): full_query = lax.all_gather(query_part, 'ctx', axis=2, tiled=True)  47.9 us
    add x31, other arithmetic, combine_parts(): first_sum * first_factor[..., None] + second_sum * second_factor[..., None]  47.2 us
    all_gather x2, blocking collectives, joined(): pieces = jax.tree.map(lambda part: lax.all_gather(part, axis), value)  45.5 us
    slice x3, local copies, waits for them, and re-layouts, joined(): tail = jax.tree.map(lambda part: part[1:], pieces)  23.6 us
    dot_general x1, matrix products, local(): jnp.dot(prefill_hidden, lax.all_gather(kv_down, 'ctx', axis=0, tiled=True...  13.4 us
    all_to_all x1, starting transfers between devices, local(): lax.all_to_all(packed, ('role', 'ctx'), split_axis=0, concat_axis=0, tile...  8.16 us
  transfers between devices with their start and end apart: 3, of which 2 were waited for; matrix products, arithmetic and copies ran while one was open for 5% of the time, Pallas kernels for 0%

commit v1 on v0

v1 whole, which is shorter than its diff:
```python
import functools
import math

import jax
import jax.numpy as jnp
from jax import lax
from jax.experimental import pallas as pl
from jax.experimental.pallas import tpu as pltpu
from jax.sharding import PartitionSpec as P

LATENT = 512
PAGE = 4
LOW = -1e30
FLOOR = -1e29
TAIL = 640


def place():
    role = lax.axis_index("role")
    ctx = lax.axis_index("ctx")
    return role, ctx // 8, (ctx // 2) % 4, ctx % 2


def ctx_of(z, y, core):
    return (z * 4 + y) * 2 + core


def gather_kernel(
    hidden_hbm,
    kv_hbm,
    gain_ref,
    query_ref,
    rows_ref,
    queries_ref,
    hidden,
    weights,
    total,
    load_sem,
    kv_send,
    kv_recv,
    pair_send,
    pair_recv,
    q_send,
    q_recv,
    q_pair_send,
    q_pair_recv,
):
    x, z, y, core = place()
    depth = kv_hbm.shape[0]
    half = depth // 2
    chunk = depth * 8

    barrier = pltpu.get_barrier_semaphore()
    others = [{"ctx": ctx_of(z, y, 1 - core)}]
    for step in (1, 2, 3):
        others.append({"ctx": ctx_of((z + step) % 4, y, core)})
        others.append({"ctx": ctx_of(z, (y + step) % 4, core)})
        others.append({"role": (x + step) % 4})
    for other in others:
        pl.semaphore_signal(barrier, inc=1, device_id=other, device_id_type=pl.DeviceIdType.MESH)

    line = [z, (z + 3) % 4, (z + 1) % 4, (z + 2) % 4]
    loads = []
    for index in range(4):
        columns = pl.ds(pl.multiple_of(line[index] * chunk, 128), chunk)
        load = pltpu.make_async_copy(
            hidden_hbm.at[:, columns], hidden.at[:, columns], load_sem.at[index]
        )
        loads.append(load)
    own_rows = pl.ds(pl.multiple_of(ctx_of(z, y, core) * depth, 16), depth)
    own_load = pltpu.make_async_copy(kv_hbm, weights.at[own_rows, :], load_sem.at[4])
    own_load.start()
    queries_ref[x, z, y, core] = query_ref[...]
    own_load.wait()
    loads[0].start()
    pl.semaphore_wait(barrier, len(others))

    def piece(z_at, y_at, core_at, part):
        start = ctx_of(z_at, y_at, core_at) * depth + part * half
        return weights.at[pl.ds(pl.multiple_of(start, 16), half), :]

    def spot(part, first, second):
        return (second, first) if part == 0 else (first, second)

    mine = [(y, z), (z, y)]
    sends = []

    def send(part, slot, where, target):
        ref = piece(*spot(part, *where), core, part)
        copy = pltpu.make_async_remote_copy(
            src_ref=ref,
            dst_ref=ref,
            send_sem=kv_send.at[part, slot],
            recv_sem=kv_recv.at[part, slot],
            device_id={"ctx": ctx_of(*spot(part, *target), core)},
            device_id_type=pl.DeviceIdType.MESH,
        )
        copy.start()
        sends.append(copy)

    def pair(part, slot, where, core_at):
        ref = piece(*spot(part, *where), core_at, part)
        return pltpu.make_async_remote_copy(
            src_ref=ref,
            dst_ref=ref,
            send_sem=pair_send.at[part, slot],
            recv_sem=pair_recv.at[part, slot],
            device_id={"ctx": ctx_of(z, y, 1 - core)},
            device_id_type=pl.DeviceIdType.MESH,
        )

    def wait_recv(part, slot, where):
        ref = piece(*spot(part, *where), core, part)
        pltpu.make_async_remote_copy(
            src_ref=ref,
            dst_ref=ref,
            send_sem=kv_send.at[part, slot],
            recv_sem=kv_recv.at[part, slot],
            device_id={"ctx": ctx_of(z, y, 1 - core)},
            device_id_type=pl.DeviceIdType.MESH,
        ).wait_recv()

    def places(part):
        first, second = mine[part]
        along = [first, (first + 3) % 4, (first + 1) % 4, (first + 2) % 4]
        found = {15: (first, second), 0: (along[1], second), 1: (along[2], second), 2: (along[3], second)}
        for index in range(4):
            found[3 + index] = (along[index], (second + 3) % 4)
            found[7 + index] = (along[index], (second + 1) % 4)
            found[11 + index] = (along[index], (second + 2) % 4)
        return found

    table = [places(0), places(1)]

    def pass_on(part, slot):
        copy = pair(part, slot, table[part][slot], core)
        copy.start()
        sends.append(copy)

    def spread(part, index):
        first, second = mine[part]
        where = table[part][(15, 0, 1, 2)[index]]
        send(part, 3 + index, where, (first, (second + 1) % 4))
        send(part, 7 + index, where, (first, (second + 3) % 4))

    def event(part, slot):
        first, second = mine[part]
        where = table[part][slot]
        wait_recv(part, slot, where)
        if slot == 1:
            turn = 1 - 2 * core
            send(part, 2, ((first - turn + 4) % 4, second), ((first + turn + 4) % 4, second))
        if 11 > slot >= 3:
            index = (slot - 3) % 4
            if slot < 7 and index in (0, 3):
                send(part, 11 + index, where, (first, (second + 1) % 4))
            if slot >= 7 and index in (1, 2):
                send(part, 11 + index, where, (first, (second + 3) % 4))
        if slot < 3:
            spread(part, slot + 1)
        pass_on(part, slot)

    q_sends = []

    def q_block(stage, z_at, y_at, x_at):
        if stage == 0:
            return queries_ref.at[x, z_at, y, core]
        if stage == 1:
            return queries_ref.at[x, :, y_at, core]
        return queries_ref.at[x_at, :, :, core]

    def q_copy(stage, step, sending):
        sign = 0 if sending else 4 - step
        at = [(v + sign) % 4 for v in (z, y, x)]
        ref = q_block(stage, *at)
        target = [
            {"ctx": ctx_of((z + step) % 4, y, core)},
            {"ctx": ctx_of(z, (y + step) % 4, core)},
            {"role": (x + step) % 4},
        ][stage]
        return pltpu.make_async_remote_copy(
            src_ref=ref,
            dst_ref=ref,
            send_sem=q_send.at[stage, step],
            recv_sem=q_recv.at[stage, step],
            device_id=target,
            device_id_type=pl.DeviceIdType.MESH,
        )

    def q_start(stage):
        for step in (1, 3, 2):
            copy = q_copy(stage, step, True)
            copy.start()
            q_sends.append(copy)

    def q_wait(stage):
        for step in (1, 3, 2):
            q_copy(stage, step, False).wait_recv()

    def q_pair(step, core_at):
        ref = queries_ref.at[(x + step) % 4, :, :, core_at]
        return pltpu.make_async_remote_copy(
            src_ref=ref,
            dst_ref=ref,
            send_sem=q_pair_send.at[step],
            recv_sem=q_pair_recv.at[step],
            device_id={"ctx": ctx_of(z, y, 1 - core)},
            device_id_type=pl.DeviceIdType.MESH,
        )

    def q_pass(step):
        copy = q_pair(step, core)
        copy.start()
        q_sends.append(copy)

    def multiply(index, tile):
        if tile == 0:
            slots = [
                (0, (15, 0, 1, 2)),
                (0, (3, 4, 5, 6)),
                (0, (7, 8, 9, 10)),
                (0, (11, 12, 13, 14)),
            ][index], (1, ((15, 0, 1, 2)[index], 3 + index, 7 + index, 11 + index))
            for part, group in slots:
                for slot in group:
                    pair(part, slot, table[part][slot], 1 - core).wait_recv()
            loads[index].wait()
        columns = pl.ds(pl.multiple_of(line[index] * chunk, 128), chunk)
        down = pl.ds(pl.multiple_of(line[index] * chunk, 16), chunk)
        span = pl.ds(tile * 256, 256)
        product = jnp.dot(
            hidden[span, columns], weights[down, :], preferred_element_type=jnp.float32
        )
        if index == 0:
            total[span, :] = product
        else:
            total[span, :] += product

    for part in (0, 1):
        first, second = mine[part]
        send(part, 0, (first, second), ((first + 1) % 4, second))
        send(part, 1, (first, second), ((first + 3) % 4, second))
    q_start(0)
    for part in (0, 1):
        pass_on(part, 15)
        spread(part, 0)
    for load in loads[1:]:
        load.start()
    for slot in (0, 1):
        for part in (0, 1):
            event(part, slot)
    q_wait(0)
    q_start(1)
    for slot in (3, 7, 2):
        for part in (0, 1):
            event(part, slot)
    q_wait(1)
    q_start(2)
    q_pass(0)
    plan = [
        (11,), (4,), (0, 0), (8,), (0, 1), (5,), (0, 2), (9,), (0, 3), (6,), (10,), (12,), (1, 0), (13,), (1, 1), (14,),
        (1, 2), (1, 3), (2, 0), (2, 1), (2, 2), (2, 3), (3, 0), (3, 1), (3, 2), (3, 3),
    ]
    for entry in plan:
        if len(entry) == 1:
            for part in (0, 1):
                event(part, entry[0])
        else:
            multiply(*entry)
    q_wait(2)
    for step in (1, 2, 3):
        q_pass(step)

    for tile in range(4):
        span = pl.ds(tile * 256, 256)
        latent = total[span, :LATENT]
        inverse = lax.rsqrt(jnp.mean(latent * latent, axis=-1, keepdims=True) + 1e-06)
        rows_ref[span, :LATENT] = (latent * inverse * gain_ref[...]).astype(jnp.bfloat16)
        rows_ref[span, LATENT:] = total[span, LATENT:].astype(jnp.bfloat16)

    for step in range(4):
        q_pair(step, 1 - core).wait_recv()
    for copy in sends + q_sends:
        copy.wait_send()


def compress(prefill_hidden, kv_down, kv_gain, query_part):
    rows, width = prefill_hidden.shape[0], kv_down.shape[1]
    vmem = pl.BlockSpec(memory_space=pltpu.VMEM)
    hbm = pl.BlockSpec(memory_space=pl.ANY)
    return pl.pallas_call(
        gather_kernel,
        out_shape=(
            jax.ShapeDtypeStruct((rows, width), jnp.bfloat16),
            jax.ShapeDtypeStruct((4, 4, 4, 2) + query_part.shape, jnp.bfloat16),
        ),
        in_specs=[hbm, hbm, vmem, vmem],
        out_specs=(vmem, vmem),
        scratch_shapes=[
            pltpu.VMEM(prefill_hidden.shape, jnp.bfloat16),
            pltpu.VMEM((prefill_hidden.shape[1], width), jnp.bfloat16),
            pltpu.VMEM((rows, width), jnp.float32),
            pltpu.SemaphoreType.DMA((5,)),
            pltpu.SemaphoreType.DMA((2, 15)),
            pltpu.SemaphoreType.DMA((2, 15)),
            pltpu.SemaphoreType.DMA((2, 16)),
            pltpu.SemaphoreType.DMA((2, 16)),
            pltpu.SemaphoreType.DMA((3, 4)),
            pltpu.SemaphoreType.DMA((3, 4)),
            pltpu.SemaphoreType.DMA((4,)),
            pltpu.SemaphoreType.DMA((4,)),
        ],
        compiler_params=pltpu.CompilerParams(
            collective_id=0, has_side_effects=True, vmem_limit_bytes=60 * 2**20
        ),
    )(prefill_hidden, kv_down, kv_gain.reshape(1, -1), query_part)


def chip_device(chip, core):
    return {"role": chip // 16, "ctx": (chip % 16) * 2 + core}


def join_kernel(
    scale,
    queries_ref,
    rows_ref,
    cache_ref,
    owner_ref,
    length_ref,
    up_ref,
    out_ref,
    partial,
    pair_in,
    outgoing,
    arrived,
    pair_send,
    pair_recv,
    send_sem,
    recv_sem,
    local_sem,
):
    x, z, y, core = place()
    chip = x * 16 + z * 4 + y
    barrier = pltpu.get_barrier_semaphore()

    @pl.loop(1, 64)
    def _(step):
        pl.semaphore_signal(
            barrier,
            inc=1,
            device_id=chip_device((chip + step) % 64, core),
            device_id_type=pl.DeviceIdType.MESH,
        )

    sibling = {"ctx": ctx_of(z, y, 1 - core)}
    pl.semaphore_signal(barrier, inc=1, device_id=sibling, device_id_type=pl.DeviceIdType.MESH)

    def queries_of(group, request):
        block = queries_ref[group].reshape(32, 16, 576).astype(jnp.float32)
        return block[:, request * 8 : request * 8 + 8].reshape(256, 576).astype(jnp.bfloat16)

    def attend(queries, keys, live):
        scores = lax.dot_general(
            queries, keys, (((1,), (1,)), ((), ())), preferred_element_type=jnp.float32
        )
        scores = jnp.where(live, scores * scale, LOW)
        best = jnp.maximum(jnp.max(scores, axis=1, keepdims=True), FLOOR)
        weight = jnp.exp2(scores - best)
        amount = jnp.sum(weight, axis=1, keepdims=True)
        summed = jnp.dot(
            weight.astype(jnp.bfloat16), keys[:, :LATENT], preferred_element_type=jnp.float32
        )
        return best, amount, summed

    def pack(block, mark):
        head = mark.astype(jnp.bfloat16).astype(jnp.float32)
        rest = mark - head
        middle = rest.astype(jnp.bfloat16).astype(jnp.float32)
        last = rest - middle
        lane = lax.broadcasted_iota(jnp.int32, mark.shape[:-1] + (TAIL - LATENT,), mark.ndim - 1)
        tail = jnp.where(lane == 0, head, jnp.where(lane == 1, middle, jnp.where(lane == 2, last, 0.0)))
        return block.astype(jnp.bfloat16), tail.astype(jnp.bfloat16)

    def mark_of(tail):
        return jnp.sum(tail.astype(jnp.float32), axis=-1, keepdims=True)

    def compute(step, group, with_cache):
        blocks, marks = [], []
        for request in (0, 1):
            queries = queries_of(group, request)
            live = owner_ref[...] == group * 2 + request
            best, amount, summed = attend(queries, rows_ref[...], live)
            if with_cache:
                keys = cache_ref[request]
                slots = keys.shape[0]
                first = ctx_of(z, y, core) * slots
                position = first + lax.broadcasted_iota(jnp.int32, (1, slots), 1)
                old_best, old_amount, old_summed = attend(
                    queries, keys, position < length_ref[request]
                )
                new_best = jnp.maximum(best, old_best)
                factor, old_factor = jnp.exp2(best - new_best), jnp.exp2(old_best - new_best)
                amount = amount * factor + old_amount * old_factor
                summed = summed * factor + old_summed * old_factor
                best = new_best
            some = amount > 0.0
            amount = jnp.where(some, amount, 1.0)
            mark = jnp.where(some, best + jnp.log2(amount), LOW)
            blocks.append((summed / amount).reshape(32, 8, LATENT))
            marks.append(mark.reshape(32, 8, 1))
        block, tail = pack(jnp.concatenate(blocks, axis=1), jnp.concatenate(marks, axis=1))
        partial[step, :, :, :, :LATENT] = block.reshape(16, 2, 16, LATENT)
        partial[step, :, :, :, LATENT:] = tail.reshape(16, 2, 16, TAIL - LATENT)

    def pair_copy(step):
        return pltpu.make_async_remote_copy(
            src_ref=partial.at[step, :, 1 - core],
            dst_ref=pair_in.at[step],
            send_sem=pair_send.at[step],
            recv_sem=pair_recv.at[step],
            device_id=sibling,
            device_id_type=pl.DeviceIdType.MESH,
        )

    def message(step, group, turn):
        spot = (z * 4 + y + turn) % 16
        return pltpu.make_async_remote_copy(
            src_ref=outgoing.at[step, spot],
            dst_ref=arrived.at[chip],
            send_sem=send_sem.at[step, turn],
            recv_sem=recv_sem.at[chip],
            device_id=chip_device(group * 16 + spot, core),
            device_id_type=pl.DeviceIdType.MESH,
        )

    def finish(step, group, first_turn):
        pair_copy(step).wait_recv()
        one = partial.at[step, :, core]
        two = pair_in.at[step]
        one_mark, two_mark = mark_of(one[:, :, LATENT:]), mark_of(two[:, :, LATENT:])
        best = jnp.maximum(one_mark, two_mark)
        one_weight, two_weight = jnp.exp2(one_mark - best), jnp.exp2(two_mark - best)
        amount = one_weight + two_weight
        block = one[:, :, :LATENT].astype(jnp.float32) * (one_weight / amount) + two[
            :, :, :LATENT
        ].astype(jnp.float32) * (two_weight / amount)
        block, tail = pack(block, jnp.maximum(best + jnp.log2(amount), LOW))
        outgoing[step, :, :, :LATENT] = block
        outgoing[step, :, :, LATENT:] = tail

        @pl.loop(first_turn, 16)
        def _(turn):
            message(step, group, turn).start()

    for step in range(4):
        group = (x + 1 + step) % 4
        compute(step, group, step == 3)
        if step == 0:
            pl.semaphore_wait(barrier, 64)
        pair_copy(step).start()
        if step > 0:
            finish(step - 1, (x + step) % 4, 0)
    finish(3, x, 1)
    own = pltpu.make_async_copy(outgoing.at[3, z * 4 + y], arrived.at[chip], local_sem)
    own.start()
    own.wait()

    @pl.loop(1, 64)
    def _(step):
        source = (chip + step) % 64
        pltpu.make_async_remote_copy(
            src_ref=arrived.at[source],
            dst_ref=arrived.at[source],
            send_sem=send_sem.at[0, 0],
            recv_sem=recv_sem.at[source],
            device_id=sibling,
            device_id_type=pl.DeviceIdType.MESH,
        ).wait_recv()

    marks = mark_of(arrived[:, :, LATENT:])
    best = jnp.max(marks, axis=0, keepdims=True)
    weight = jnp.exp2(marks - best)
    amount = jnp.sum(weight, axis=0)
    summed = jnp.sum(arrived[:, :, :LATENT].astype(jnp.float32) * weight, axis=0)
    latent = (summed / amount).astype(jnp.bfloat16)
    heads = up_ref.shape[0]
    row = lax.broadcasted_iota(jnp.int32, (16, 1), 0) % heads
    result = jnp.zeros(out_ref.shape, jnp.float32)
    for head in range(heads):
        product = jnp.dot(latent, up_ref[head], preferred_element_type=jnp.float32)
        result = jnp.where(row == head, product, result)
    out_ref[...] = result.astype(jnp.bfloat16)

    for step in range(4):
        pair_copy(step).wait_send()

        @pl.loop(1 if step == 3 else 0, 16)
        def _(turn):
            message(step, (x + 1 + step) % 4, turn).wait_send()


def join(queries, rows, cache, owner, lengths, value_up, scale):
    vmem = pl.BlockSpec(memory_space=pltpu.VMEM)
    smem = pl.BlockSpec(memory_space=pltpu.SMEM)
    return pl.pallas_call(
        functools.partial(join_kernel, scale),
        out_shape=jax.ShapeDtypeStruct((16, value_up.shape[2]), jnp.bfloat16),
        in_specs=[vmem, vmem, vmem, vmem, smem, vmem],
        out_specs=vmem,
        scratch_shapes=[
            pltpu.VMEM((4, 16, 2, 16, TAIL), jnp.bfloat16),
            pltpu.VMEM((4, 16, 16, TAIL), jnp.bfloat16),
            pltpu.VMEM((4, 16, 16, TAIL), jnp.bfloat16),
            pltpu.VMEM((64, 16, TAIL), jnp.bfloat16),
            pltpu.SemaphoreType.DMA((4,)),
            pltpu.SemaphoreType.DMA((4,)),
            pltpu.SemaphoreType.DMA((4, 16)),
            pltpu.SemaphoreType.DMA((64,)),
            pltpu.SemaphoreType.DMA,
        ],
        compiler_params=pltpu.CompilerParams(
            collective_id=1, has_side_effects=True, vmem_limit_bytes=60 * 2**20
        ),
    )(queries, rows, cache, owner, lengths, value_up)


def local(
    prefill_hidden,
    kv_down,
    kv_gain,
    q_nope,
    q_rope,
    key_up,
    value_up,
    latent_cache,
    cache_len,
    page_list,
):
    count_ctx = lax.axis_size("ctx")
    role_index = lax.axis_index("role")
    my_device = role_index * count_ctx + lax.axis_index("ctx")
    req_grp = q_nope.shape[0]
    pages_dev = prefill_hidden.shape[0] // PAGE
    scale = math.log2(math.e) / math.sqrt(q_nope.shape[3] + q_rope.shape[3])
    absorbed = jnp.einsum(
        "rthn,hnc->rthc", q_nope, key_up, preferred_element_type=jnp.float32
    ).astype(jnp.bfloat16)
    query_part = jnp.concatenate([absorbed, q_rope], axis=-1)
    query_part = query_part.reshape(-1, query_part.shape[-1])
    rows, queries = compress(prefill_hidden, kv_down, kv_gain, query_part)
    bins = lax.dynamic_slice_in_dim(page_list[:, 0], my_device * pages_dev, pages_dev)
    request = bins // (req_grp * count_ctx) * req_grp + bins % req_grp
    owner = jnp.repeat(request, PAGE)[None, :]
    lengths = lax.dynamic_slice_in_dim(cache_len, role_index * req_grp, req_grp)
    out = join(queries, rows, latent_cache, owner, lengths, value_up, scale)
    return out.reshape(q_nope.shape[:3] + (value_up.shape[2],))


def solution(mesh):
    return jax.shard_map(
        local,
        mesh=mesh,
        in_specs=(
            P(("role", "ctx"), None),
            P("ctx", None),
            P(),
            P("role", None, "ctx", None),
            P("role", None, "ctx", None),
            P("ctx", None, None),
            P("ctx", None, None),
            P("role", "ctx", None),
            P(),
            P(),
        ),
        out_specs=P("role", None, "ctx", None),
        check_vma=False,
    )
```

time: 363 us -> 102 us (0.28)
  waiting for transfers between devices: 122 us -> 0 us
  blocking collectives: 93.4 us -> 0 us
  Pallas kernels: 0 us -> 91.9 us
  other arithmetic: 55.6 us -> 0.04 us
  local copies, waits for them, and re-layouts: 42.4 us -> 8 us
  matrix products: 23.8 us -> 0.86 us
  between operations: 13.8 us -> 0.05 us
  starting transfers between devices: 8.21 us -> 0 us
    all_gather x2 -> x0, waiting for transfers between devices: 122 us -> none  [the longest x1 65.4 us: joined(): pieces = jax.tree.map(lambda part: lax.all_gather(part, axis), value)]
    all_gather x3 -> x0, blocking collectives: 93.4 us -> none  [the longest x1 47.9 us: local(): full_query = lax.all_gather(query_part, 'ctx', axis=2, tiled=True)]
    pallas_call x0 -> x2, Pallas kernels: none -> 91.9 us  [the longest x1 55.1 us: compress(): pl.pallas_call(gather_kernel, out_shape=(jax.ShapeDtypeStruct((rows, widt...]
    add x66 -> x1, other arithmetic: 48.1 us -> 0.01 us  [local(): request = bins // (req_grp * count_ctx) * req_grp + bins % req_grp]
    slice x13 -> x0, local copies, waits for them, and re-layouts: 26.8 us -> none  [the longest x3 23.6 us: joined(): tail = jax.tree.map(lambda part: part[1:], pieces)]
    dot_general x11 -> x0, matrix products: 23.6 us -> none  [the longest x1 13.4 us: local(): jnp.dot(prefill_hidden, lax.all_gather(kv_down, 'ctx', axis=0, tiled=True...]
    all_to_all x1 -> x0, starting transfers between devices: 8.16 us -> none  [local(): lax.all_to_all(packed, ('role', 'ctx'), split_axis=0, concat_axis=0, tile...]
  transfers between devices with their start and end apart: 3 -> 0, of which waited for: 2 -> 0; matrix products, arithmetic and copies ran while one was open for 5% -> 0% of each run, Pallas kernels for 0% -> 0%
where the time goes in v1:
time: 102 us; the launch traced here: 101 us
  Pallas kernels  91.9 us (90%)
  local copies, waits for them, and re-layouts  8 us (8%)
    pallas_call x1, Pallas kernels, compress(): pl.pallas_call(gather_kernel, out_shape=(jax.ShapeDtypeStruct((rows, widt...  55.1 us
    pallas_call x1, Pallas kernels, join(): pl.pallas_call(functools.partial(join_kernel, scale), out_shape=jax.Shape...  36.8 us
    unnamed x7, local copies, waits for them, and re-layouts  4.57 us

profile of v1, /device:TPU:0, one launch (start us, length us, event | category | flops | bytes accessed | tf_op | source)
XLA Modules:
  0.0 100.9 jit_solution(9523083373722491472)
XLA Ops:
  0.0 0.0 copy-start
  0.0 0.7 constant_dynamic-slice_fusion
  0.8 0.1 broadcast_in_dim.3
  0.9 0.7 broadcast_in_dim_reshape.3.owner_ref
  1.6 1.2 %dynamic_slice.10.length_ref = s32[2]{0:T(128)} dynamic-slice(s32[8]{0:T(128)} %param.18, s32[]{:T(128)S(6)} %select_n.21), dynamic_slice_sizes={2} | dynamic-slice | bytes 20 | tf_op jit(solution)/shard_map/dynamic_slice | solution.py:554
  2.8 0.0 copy-done
  2.8 0.9 fusion
  3.7 0.7 copy.16
  4.4 0.6 reshape.11.query_ref
  5.1 0.0 copy-start.1
  5.1 55.1 %shard_map.100 = (bf16[1024,576]{1,0:T(8,128)(2,1)}, bf16[4,4,4,2,16,576]{5,4,3,2,1,0:T(8,128)(2,1)}) custom-call(bf16[1024,7168]{1,0:T(8,128)(2,1)} %hidden_hbm.1, bf16[224,576]{1,0:T(8,128)(2,1)} %kv_hbm.1, f32[1,512]{1,0:T(1,128)} %bitcast.12, bf16[16,576]{1,0:T(8,128)(2,1)} %reshape.11.query_ref), custom_call_target="tpu_custom_call" | custom-call | tf_op jit(solution)/shard_map/pallas_call | solution.py:291
  60.2 0.0 copy-done.1
  60.2 2.6 %copy.18.cache_ref = bf16[2,1024,576]{2,1,0:T(8,128)(2,1)} copy(bf16[2,1024,576]{1,2,0:T(8,128)(2,1)S(1)} %copy-done.1) | data formatting | bytes 4718592 | tf_op args[7]
  62.8 36.8 %shard_map.101 = bf16[16,128]{1,0:T(8,128)(2,1)} custom-call(bf16[4,4,4,2,16,576]{5,4,3,2,1,0:T(8,128)(2,1)} %get-tuple-element.7.queries_ref, bf16[1024,576]{1,0:T(8,128)(2,1)} %get-tuple-element.8.rows_ref, bf16[2,1024,576]{2,1,0:T(8,128)(2,1)} %copy.18.cache_ref, s32[1,1024]{1,0:T(1,128)} %broadcast_in_dim_reshape.3.owner_ref, ...), custom_call_target="tpu_custom_call" | custom-call | tf_op jit(solution)/shard_map/pallas_call | solution.py:505
  99.6 1.3 %copy.23 = bf16[2,2,4,128]{3,2,1,0:T(4,128)(2,1)} copy(bf16[2,2,4,128]{3,2,1,0:T(4,128)(2,1)} %bitcast.10) | data formatting | bytes 8192
  (3 shorter events, 0.0 us)
Async XLA Ops:
  0.0 2.8 %copy-start = (bf16[4,128,512]{2,1,0:T(8,128)(2,1)S(1)}, bf16[4,128,512]{2,1,0:T(8,128)(2,1)}, u32[]{:S(2)}) copy-start(bf16[4,128,512]{2,1,0:T(8,128)(2,1)} %param.15) | copy-start | bytes 1572868
  5.1 55.1 %copy-start.1 = (bf16[2,1024,576]{1,2,0:T(8,128)(2,1)S(1)}, bf16[2,1024,576]{1,2,0:T(8,128)(2,1)}, u32[]{:S(2)}) copy-start(bf16[2,1024,576]{1,2,0:T(8,128)(2,1)} %param.17) | copy-start | bytes 7077892

commit v2 on v0

v2 whole, which is shorter than its diff:
```python
import functools
import math

import jax
import jax.numpy as jnp
from jax import lax
from jax.experimental import pallas as pl
from jax.experimental.pallas import tpu as pltpu
from jax.sharding import PartitionSpec as P

LATENT = 512
PAGE = 4
LOW = -1e30
FLOOR = -1e29
TAIL = 640
MESH = pl.DeviceIdType.MESH
TURNS = (2, 1, 3, 0)
ONWARD = (0, 1)
PLAN = (
    ("q", 0), ("q", 1), ("p", 0, 0), ("p", 1, 0), ("p", 0, 1), ("p", 0, 2), ("o", 0), ("o", 1), ("q", 2),
    ("n", 1, 0), ("p", 1, 1), ("n", 0, 0), ("p", 1, 2), ("c",), ("p", 0, 3), ("n", 1, 2), ("n", 1, 1), ("n",
    0, 1), ("n", 0, 2), ("p", 1, 3), ("n", 0, 3), ("k", 0), ("m", 0, 0), ("m", 0, 1), ("m", 0, 2), ("m", 2,
    0), ("m", 2, 1), ("n", 1, 3), ("m", 0, 3), ("k", 1), ("m", 2, 2), ("m", 2, 3), ("m", 1, 0), ("m", 1, 1),
    ("m", 1, 2), ("m", 1, 3), ("m", 3, 0), ("m", 3, 1), ("m", 3, 2), ("m", 3, 3),
)


def place():
    role = lax.axis_index("role")
    ctx = lax.axis_index("ctx")
    return role, ctx // 8, (ctx // 2) % 4, ctx % 2


def ctx_of(z, y, core):
    return (z * 4 + y) * 2 + core


def remote(src, dst, send_sem, recv_sem, device):
    return pltpu.make_async_remote_copy(
        src_ref=src,
        dst_ref=dst,
        send_sem=send_sem,
        recv_sem=recv_sem,
        device_id=device,
        device_id_type=MESH,
    )


def pack(block, mark):
    head = mark.astype(jnp.bfloat16).astype(jnp.float32)
    rest = mark - head
    middle = rest.astype(jnp.bfloat16).astype(jnp.float32)
    last = rest - middle
    lane = lax.broadcasted_iota(jnp.int32, mark.shape[:-1] + (TAIL - LATENT,), mark.ndim - 1)
    tail = jnp.where(lane == 0, head, jnp.where(lane == 1, middle, jnp.where(lane == 2, last, 0.0)))
    return block.astype(jnp.bfloat16), tail.astype(jnp.bfloat16)


def mark_of(tail):
    return jnp.sum(tail.astype(jnp.float32), axis=-1, keepdims=True)


def joined(parts):
    marks = [mark_of(part[..., LATENT:]) for part in parts]
    best = functools.reduce(jnp.maximum, marks)
    weights = [jnp.exp2(mark - best) for mark in marks]
    amount = functools.reduce(jnp.add, weights)
    block = functools.reduce(
        jnp.add, [part[..., :LATENT].astype(jnp.float32) * w for part, w in zip(parts, weights)]
    )
    return block / amount, jnp.maximum(best + jnp.log2(amount), LOW)


def attend(queries, blocks, scale):
    scores = []
    for keys, live, flipped in blocks:
        inner = (0,) if flipped else (1,)
        score = lax.dot_general(
            queries, keys, (((1,), inner), ((), ())), preferred_element_type=jnp.float32
        )
        scores.append(jnp.where(live, score * scale, LOW))
    best = functools.reduce(
        jnp.maximum, [jnp.max(score, axis=1, keepdims=True) for score in scores]
    )
    best = jnp.maximum(best, FLOOR)
    amount, summed = 0.0, 0.0
    for score, (keys, _, flipped) in zip(scores, blocks):
        weight = jnp.exp2(score - best)
        amount = amount + jnp.sum(weight, axis=1, keepdims=True)
        latent, outer = (keys[:LATENT, :], (1,)) if flipped else (keys[:, :LATENT], (0,))
        summed = summed + lax.dot_general(
            weight.astype(jnp.bfloat16),
            latent,
            (((1,), outer), ((), ())),
            preferred_element_type=jnp.float32,
        )
    return best, amount, summed


def merge_two(first, second):
    best = jnp.maximum(first[0], second[0])
    one, two = jnp.exp2(first[0] - best), jnp.exp2(second[0] - best)
    return best, first[1] * one + second[1] * two, first[2] * one + second[2] * two


def kernel(
    scale,
    hidden_hbm,
    kv_hbm,
    gain_ref,
    nope_ref,
    rope_ref,
    key_up_ref,
    value_up_hbm,
    cache_hbm,
    length_ref,
    page_hbm,
    out_ref,
    hidden,
    weights,
    total,
    rows,
    queries,
    cache,
    value_up,
    pages,
    owner,
    old_best,
    old_amount,
    old_summed,
    outgoing,
    arrived,
    second,
    second_in,
    third,
    third_in,
    load_sem,
    kv_send,
    kv_recv,
    pair_send,
    pair_recv,
    q_send,
    q_recv,
    cache_send,
    cache_recv,
    rows_send,
    rows_recv,
    one_send,
    one_recv,
    two_send,
    two_recv,
    three_send,
    three_recv,
):
    x, z, y, core = place()
    depth = kv_hbm.shape[0]
    half = depth // 2
    chunk = depth * 8
    sibling = {"ctx": ctx_of(z, y, 1 - core)}

    barrier = pltpu.get_barrier_semaphore()
    pl.semaphore_signal(barrier, inc=1, device_id=sibling, device_id_type=MESH)
    for step in (1, 2, 3):
        for device in (
            {"role": (x + step) % 4},
            {"ctx": ctx_of((z + step) % 4, y, core)},
            {"ctx": ctx_of(z, (y + step) % 4, core)},
        ):
            pl.semaphore_signal(barrier, inc=1, device_id=device, device_id_type=MESH)

    line = [z, (z + 3) % 4, (z + 1) % 4, (z + 2) % 4]
    own_rows = pl.ds(pl.multiple_of(ctx_of(z, y, core) * depth, 16), depth)
    own_load = pltpu.make_async_copy(kv_hbm, weights.at[own_rows, :], load_sem.at[4])
    own_load.start()
    loads = []
    for index in range(4):
        columns = pl.ds(pl.multiple_of(line[index] * chunk, 128), chunk)
        loads.append(
            pltpu.make_async_copy(
                hidden_hbm.at[:, columns], hidden.at[:, columns], load_sem.at[index]
            )
        )
    page_start = pl.multiple_of((x * 16 + z * 4 + y) * pages.shape[1], 128)
    others = [
        pltpu.make_async_copy(
            page_hbm.at[:, pl.ds(page_start, pages.shape[1])], pages, load_sem.at[5]
        ),
        pltpu.make_async_copy(cache_hbm, cache.at[core], load_sem.at[6]),
        pltpu.make_async_copy(value_up_hbm, value_up, load_sem.at[7]),
    ]

    heads = key_up_ref.shape[0]
    row = lax.broadcasted_iota(jnp.int32, (16, 1), 0) % heads

    nope = jnp.concatenate(
        [nope_ref[r, t].astype(jnp.float32) for r in (0, 1) for t in (0, 1)], axis=0
    ).astype(jnp.bfloat16)
    rope = jnp.concatenate(
        [rope_ref[r, t].astype(jnp.float32) for r in (0, 1) for t in (0, 1)], axis=0
    )
    absorbed = jnp.zeros((16, LATENT), jnp.float32)
    for head in range(heads):
        product = jnp.dot(nope, key_up_ref[head], preferred_element_type=jnp.float32)
        absorbed = jnp.where(row == head, product, absorbed)
    queries[x, z, y, core, :, :LATENT] = absorbed.astype(jnp.bfloat16)
    queries[x, z, y, core, :, LATENT:] = rope.astype(jnp.bfloat16)
    own_load.wait()
    pl.semaphore_wait(barrier, 10)

    def piece(z_at, y_at, core_at, part):
        start = ctx_of(z_at, y_at, core_at) * depth + part * half
        return weights.at[pl.ds(pl.multiple_of(start, 16), half), :]

    def spot(part, first, second):
        return (second, first) if part == 0 else (first, second)

    mine = [(y, z), (z, y)]
    sends = []

    def begin(copy):
        copy.start()
        sends.append(copy)

    def send(part, slot, where, target):
        ref = piece(*spot(part, *where), core, part)
        device = {"ctx": ctx_of(*spot(part, *target), core)}
        begin(remote(ref, ref, kv_send.at[part, slot], kv_recv.at[part, slot], device))

    def pair(part, slot, where, core_at):
        ref = piece(*spot(part, *where), core_at, part)
        return remote(ref, ref, pair_send.at[part, slot], pair_recv.at[part, slot], sibling)

    def places(part):
        first, second = mine[part]
        along = [first, (first + 3) % 4, (first + 1) % 4, (first + 2) % 4]
        found = {15: (first, second)}
        for index in range(4):
            if index < 3:
                found[index] = (along[index + 1], second)
            found[3 + index] = (along[index], (second + 3) % 4)
            found[7 + index] = (along[index], (second + 1) % 4)
            found[11 + index] = (along[index], (second + 2) % 4)
        return found

    table = [places(0), places(1)]

    def pass_on(part, slot):
        begin(pair(part, slot, table[part][slot], core))

    seen = set()

    def need(part, *slots):
        for slot in slots:
            if (part, slot) not in seen and slot != 15:
                seen.add((part, slot))
                ref = piece(*spot(part, *table[part][slot]), core, part)
                remote(
                    ref, ref, kv_send.at[part, slot], kv_recv.at[part, slot], sibling
                ).wait_recv()
                pass_on(part, slot)

    def spread(part, index):
        first, second = mine[part]
        where = table[part][(15, 0, 1, 2)[index]]
        need(part, (15, 0, 1, 2)[index])
        send(part, 3 + index, where, (first, (second + 1) % 4))
        send(part, 7 + index, where, (first, (second + 3) % 4))

    def opposite(part):
        first, second = mine[part]
        turn = 1 - 2 * core
        need(part, 0, 1)
        send(part, 2, ((first - turn + 4) % 4, second), ((first + turn + 4) % 4, second))

    def onward(part, index):
        first, second = mine[part]
        slot, step = (3 + index, 1) if index in ONWARD else (7 + index, 3)
        need(part, slot)
        send(part, 11 + index, table[part][slot], (first, (second + step) % 4))

    one_at, two_at = jnp.where(core == 0, z, y), jnp.where(core == 0, y, z)

    def q_spot(first, second):
        return jnp.where(core == 0, first, second), jnp.where(core == 0, second, first)

    def q_copies(stage, step, sending):
        sign = 0 if sending else 4 - step
        if stage == 0:
            ref = queries.at[(x, *q_spot((one_at + sign) % 4, two_at), core)]
            device = {"ctx": ctx_of(*q_spot((one_at + step) % 4, two_at), core)}
            return [remote(ref, ref, q_send.at[0, step, 0], q_recv.at[0, step, 0], device)]
        if stage == 1:
            device = {"ctx": ctx_of(*q_spot(one_at, (two_at + step) % 4), core)}
            copies = []
            for index in range(4):
                ref = queries.at[
                    (x, *q_spot((one_at + index) % 4, (two_at + sign) % 4), core)
                ]
                copies.append(
                    remote(ref, ref, q_send.at[1, step, index], q_recv.at[1, step, index], device)
                )
            return copies
        ref = queries.at[(x + sign) % 4, :, :, core]
        device = {"role": (x + step) % 4}
        return [remote(ref, ref, q_send.at[2, step, 0], q_recv.at[2, step, 0], device)]

    def q_wait(stage):
        for step in (1, 3, 2):
            for copy in q_copies(stage, step, False):
                copy.wait_recv()

    def q_stage(stage):
        if stage > 0:
            q_wait(stage - 1)
        for step in (1, 3, 2):
            for copy in q_copies(stage, step, True):
                begin(copy)

    def multiply(index, tile):
        if tile == 0:
            slots = (
                (0, ((15, 0, 1, 2), (3, 4, 5, 6), (7, 8, 9, 10), (11, 12, 13, 14))[index]),
                (1, ((15, 0, 1, 2)[index], 3 + index, 7 + index, 11 + index)),
            )
            for part, group in slots:
                need(part, *group)
            for part, group in slots:
                for slot in group:
                    pair(part, slot, table[part][slot], 1 - core).wait_recv()
            loads[index].wait()
        columns = pl.ds(pl.multiple_of(line[index] * chunk, 128), chunk)
        down = pl.ds(pl.multiple_of(line[index] * chunk, 16), chunk)
        span = pl.ds(tile * 256, 256)
        product = jnp.dot(
            hidden[span, columns], weights[down, :], preferred_element_type=jnp.float32
        )
        if index == 0:
            total[span, :] = product
        else:
            total[span, :] += product

    def queries_of(group):
        return queries[group, :, :, core].reshape(256, 576)

    row_request = lax.broadcasted_iota(jnp.int32, (256, 1), 0) // 8 % 2

    def cache_pair(core_at):
        return remote(
            cache_hbm, cache.at[core_at], cache_send.at[0], cache_recv.at[0], sibling
        )

    def cached(turn):
        if turn == 0:
            others[1].wait()
        else:
            cache_pair(1 - core).wait_recv()
        source = core if turn == 0 else 1 - core
        slots = cache.shape[3]
        position = ctx_of(z, y, source) * slots + lax.broadcasted_iota(jnp.int32, (1, slots), 1)
        blocks = []
        for request in (0, 1):
            live = (position < length_ref[x * 2 + request]) & (row_request == request)
            blocks.append((cache[source, request], live, True))
        found = attend(queries_of(x), blocks, scale)
        if turn == 1:
            found = merge_two(found, (old_best[...], old_amount[...], old_summed[...]))
        old_best[...], old_amount[...], old_summed[...] = found

    for part in (0, 1):
        first, second_at = mine[part]
        send(part, 0, (first, second_at), ((first + 1) % 4, second_at))
        send(part, 1, (first, second_at), ((first + 3) % 4, second_at))
    for copy in others:
        copy.start()
    for load in loads:
        load.start()
    for part in (0, 1):
        pass_on(part, 15)

    for kind, *numbers in PLAN:
        if kind == "p":
            spread(*numbers)
        elif kind == "o":
            opposite(*numbers)
        elif kind == "n":
            onward(*numbers)
        elif kind == "q":
            q_stage(*numbers)
        elif kind == "c":
            begin(cache_pair(core))
        elif kind == "k":
            cached(*numbers)
        else:
            multiply(*numbers)

    def rows_pair(tile, core_at):
        ref = rows.at[core_at, pl.ds(tile * 256, 256), :]
        return remote(ref, ref, rows_send.at[tile], rows_recv.at[tile], sibling)

    for tile in range(4):
        span = pl.ds(tile * 256, 256)
        latent = total[span, :LATENT]
        inverse = lax.rsqrt(jnp.mean(latent * latent, axis=-1, keepdims=True) + 1e-06)
        rows[core, span, :LATENT] = (latent * inverse * gain_ref[...]).astype(jnp.bfloat16)
        rows[core, span, LATENT:] = total[span, LATENT:].astype(jnp.bfloat16)
        begin(rows_pair(tile, core))

    others[0].wait()
    bins = pages[...]
    request_of = (bins // 64 * 2 + bins % 2).astype(jnp.float32)
    count = pages.shape[1] // 2
    page = lax.broadcasted_iota(jnp.int32, (count, count * PAGE), 0)
    key = lax.broadcasted_iota(jnp.int32, (count, count * PAGE), 1)
    spread_out = (key // PAGE == page).astype(jnp.float32).astype(jnp.bfloat16)
    request_of = jnp.concatenate([request_of[:, :count], request_of[:, count:]], axis=0)
    wide = jnp.concatenate([request_of] * 4, axis=0).astype(jnp.bfloat16)
    owner[...] = jnp.dot(wide, spread_out, preferred_element_type=jnp.float32)[0:2, :]

    def compute(step):
        turn = TURNS[step]
        group = (x + turn) % 4
        if turn != 0:
            for copy in q_copies(2, 4 - turn, False):
                copy.wait_recv()
        if step == 0:
            for tile in range(4):
                rows_pair(tile, 1 - core).wait_recv()
        wanted = (group * 2 + row_request).astype(jnp.float32)
        blocks = []
        for source in (core, 1 - core):
            blocks.append((rows[source], owner[pl.ds(source, 1), :] == wanted, False))
        found = attend(queries_of(group), blocks, scale)
        if turn == 0:
            found = merge_two(found, (old_best[...], old_amount[...], old_summed[...]))
        best, amount, summed = found
        some = amount > 0.0
        amount = jnp.where(some, amount, 1.0)
        mark = jnp.where(some, best + jnp.log2(amount), LOW)
        block, tail = pack(summed / amount, mark)
        outgoing[step, :, :, :, :LATENT] = block.reshape(4, 4, 16, LATENT)
        outgoing[step, :, :, :, LATENT:] = tail.reshape(4, 4, 16, TAIL - LATENT)
        if turn != 0:

            @pl.when(core == 0)
            def _():
                out_x(step).start()

        @pl.when(core == 1)
        def _():
            for turn in (2, 1, 3):
                out_z(step, turn).start()

    def out_x(step):
        return remote(
            outgoing.at[step],
            arrived.at[step],
            one_send.at[step, 0],
            one_recv.at[step, 0],
            {"role": (x + TURNS[step]) % 4},
        )

    def out_z(step, turn):
        there = (z + turn) % 4
        return remote(
            outgoing.at[step, there],
            arrived.at[step, turn],
            one_send.at[step, turn],
            one_recv.at[step, turn],
            {"ctx": ctx_of(there, y, core)},
        )

    def next_y(turn):
        there = (y + turn) % 4
        return remote(
            second.at[:, there],
            second_in.at[turn],
            two_send.at[turn],
            two_recv.at[turn],
            {"ctx": ctx_of(z, there, core)},
        )

    def next_x(step):
        return remote(
            second.at[step],
            second_in.at[step],
            two_send.at[step],
            two_recv.at[step],
            {"role": (x + TURNS[step]) % 4},
        )

    def end_z(turn):
        there = (z + turn) % 4
        return remote(
            third.at[there],
            third_in.at[turn],
            three_send.at[turn],
            three_recv.at[turn],
            {"ctx": ctx_of(there, y, core)},
        )

    def end_y(turn):
        there = (y + turn) % 4
        return remote(
            third.at[there],
            third_in.at[turn],
            three_send.at[turn],
            three_recv.at[turn],
            {"ctx": ctx_of(z, there, core)},
        )

    def put(ref, parts):
        block, tail = pack(*joined(parts))
        ref[..., :LATENT] = block
        ref[..., LATENT:] = tail

    def merge(step):
        @pl.when(core == 1)
        def _():
            for turn in (1, 2, 3):
                out_z(step, turn).wait_recv()
            put(second.at[step], [outgoing[step, z]] + [arrived[step, turn] for turn in (1, 2, 3)])
            if TURNS[step] != 0:
                next_x(step).start()

    for step in range(4):
        compute(step)
        if step > 0:
            merge(step - 1)
    merge(3)

    def conclude(block):
        latent = block.astype(jnp.bfloat16)
        result = jnp.zeros((16, value_up.shape[2]), jnp.float32)
        for head in range(heads):
            product = jnp.dot(latent, value_up[head], preferred_element_type=jnp.float32)
            result = jnp.where(row == head, product, result)
        for index in range(4):
            out_ref[index // 2, index % 2] = result[index * 4 : index * 4 + 4].astype(jnp.bfloat16)

    others[2].wait()

    @pl.when(core == 0)
    def _():
        for step in range(3):
            out_x(step).wait_recv()
        put(second, [outgoing[3]] + [arrived[step] for step in range(3)])
        for turn in (2, 1, 3):
            next_y(turn).start()
        for turn in (1, 3, 2):
            next_y(turn).wait_recv()
        put(third, [second[:, y]] + [second_in[turn] for turn in (1, 2, 3)])
        for turn in (2, 1, 3):
            end_z(turn).start()
        for turn in (1, 3, 2):
            end_z(turn).wait_recv()
        conclude(joined([third[z]] + [third_in[turn] for turn in (1, 2, 3)])[0])
        for step in range(3):
            out_x(step).wait_send()
        for turn in (1, 2, 3):
            next_y(turn).wait_send()
            end_z(turn).wait_send()

    @pl.when(core == 1)
    def _():
        for step in range(3):
            next_x(step).wait_recv()
        put(third, [second[3]] + [second_in[step] for step in range(3)])
        for turn in (2, 1, 3):
            end_y(turn).start()
        for turn in (1, 3, 2):
            end_y(turn).wait_recv()
        conclude(joined([third[y]] + [third_in[turn] for turn in (1, 2, 3)])[0])
        for step in range(3):
            next_x(step).wait_send()
        for turn in (1, 2, 3):
            for step in range(4):
                out_z(step, turn).wait_send()
            end_y(turn).wait_send()

    for copy in sends:
        copy.wait_send()


def local(
    prefill_hidden,
    kv_down,
    kv_gain,
    q_nope,
    q_rope,
    key_up,
    value_up,
    latent_cache,
    cache_len,
    page_list,
):
    rows, width = prefill_hidden.shape[0], kv_down.shape[1]
    scale = math.log2(math.e) / math.sqrt(q_nope.shape[3] + q_rope.shape[3])
    vmem = pl.BlockSpec(memory_space=pltpu.VMEM)
    smem = pl.BlockSpec(memory_space=pltpu.SMEM)
    hbm = pl.BlockSpec(memory_space=pl.ANY)
    bf16, f32, dma = jnp.bfloat16, jnp.float32, pltpu.SemaphoreType.DMA
    flipped = jnp.swapaxes(latent_cache, 1, 2)
    return pl.pallas_call(
        functools.partial(kernel, scale),
        out_shape=jax.ShapeDtypeStruct(q_nope.shape[:3] + (value_up.shape[2],), bf16),
        in_specs=[hbm, hbm, vmem, vmem, vmem, vmem, hbm, hbm, smem, hbm],
        out_specs=vmem,
        scratch_shapes=[
            pltpu.VMEM(prefill_hidden.shape, bf16),
            pltpu.VMEM((prefill_hidden.shape[1], width), bf16),
            pltpu.VMEM((rows, width), f32),
            pltpu.VMEM((2, rows, width), bf16),
            pltpu.VMEM((4, 4, 4, 2, 16, width), bf16),
            pltpu.VMEM((2,) + flipped.shape, bf16),
            pltpu.VMEM(value_up.shape, bf16),
            pltpu.VMEM((1, 2 * rows // PAGE), jnp.int32),
            pltpu.VMEM((2, rows), f32),
            pltpu.VMEM((256, 1), f32),
            pltpu.VMEM((256, 1), f32),
            pltpu.VMEM((256, LATENT), f32),
            pltpu.VMEM((4, 4, 4, 16, TAIL), bf16),
            pltpu.VMEM((4, 4, 4, 16, TAIL), bf16),
            pltpu.VMEM((4, 4, 16, TAIL), bf16),
            pltpu.VMEM((4, 4, 16, TAIL), bf16),
            pltpu.VMEM((4, 16, TAIL), bf16),
            pltpu.VMEM((4, 16, TAIL), bf16),
            dma((8,)),
            dma((2, 15)),
            dma((2, 15)),
            dma((2, 16)),
            dma((2, 16)),
            dma((3, 4, 4)),
            dma((3, 4, 4)),
            dma((1,)),
            dma((1,)),
            dma((4,)),
            dma((4,)),
            dma((4, 4)),
            dma((4, 4)),
            dma((4,)),
            dma((4,)),
            dma((4,)),
            dma((4,)),
        ],
        compiler_params=pltpu.CompilerParams(
            collective_id=0, has_side_effects=True, vmem_limit_bytes=60 * 2**20
        ),
    )(
        prefill_hidden,
        kv_down,
        kv_gain.reshape(1, -1),
        q_nope,
        q_rope,
        key_up,
        value_up,
        flipped,
        cache_len,
        page_list.reshape(1, -1),
    )


def solution(mesh):
    return jax.shard_map(
        local,
        mesh=mesh,
        in_specs=(
            P(("role", "ctx"), None),
            P("ctx", None),
            P(),
            P("role", None, "ctx", None),
            P("role", None, "ctx", None),
            P("ctx", None, None),
            P("ctx", None, None),
            P("role", "ctx", None),
            P(),
            P(),
        ),
        out_specs=P("role", None, "ctx", None),
        check_vma=False,
    )
```

time: 363 us -> 84.7 us (0.23)
  waiting for transfers between devices: 122 us -> 0 us
  blocking collectives: 93.4 us -> 0 us
  Pallas kernels: 0 us -> 83.2 us
  other arithmetic: 55.6 us -> 0 us
  local copies, waits for them, and re-layouts: 42.4 us -> 1.28 us
  matrix products: 23.8 us -> 0 us
  between operations: 13.8 us -> 0.01 us
  starting transfers between devices: 8.21 us -> 0 us
    all_gather x2 -> x0, waiting for transfers between devices: 122 us -> none  [the longest x1 65.4 us: joined(): pieces = jax.tree.map(lambda part: lax.all_gather(part, axis), value)]
    all_gather x3 -> x0, blocking collectives: 93.4 us -> none  [the longest x1 47.9 us: local(): full_query = lax.all_gather(query_part, 'ctx', axis=2, tiled=True)]
    pallas_call x0 -> x1, Pallas kernels: none -> 83.2 us  [local(): pl.pallas_call(functools.partial(kernel, scale), out_shape=jax.ShapeDtype...]
    add x66 -> x0, other arithmetic: 48.1 us -> none  [the longest x31 47.2 us: combine_parts(): first_sum * first_factor[..., None] + second_sum * second_factor[..., None]]
    slice x13 -> x0, local copies, waits for them, and re-layouts: 26.8 us -> none  [the longest x3 23.6 us: joined(): tail = jax.tree.map(lambda part: part[1:], pieces)]
    dot_general x12 -> x0, matrix products: 23.8 us -> none  [the longest x1 13.4 us: local(): jnp.dot(prefill_hidden, lax.all_gather(kv_down, 'ctx', axis=0, tiled=True...]
    all_to_all x1 -> x0, starting transfers between devices: 8.16 us -> none  [local(): lax.all_to_all(packed, ('role', 'ctx'), split_axis=0, concat_axis=0, tile...]
    reshape x1 -> x0, local copies, waits for them, and re-layouts: 4 us -> none  [local(): packed = packed.reshape(devices, req_grp, most_pages * PAGE, width)]
  transfers between devices with their start and end apart: 3 -> 0, of which waited for: 2 -> 0; matrix products, arithmetic and copies ran while one was open for 5% -> 0% of each run, Pallas kernels for 0% -> 0%
where the time goes in v2:
time: 84.7 us; the launch traced here: 84.5 us
  Pallas kernels  83.2 us (98%)
  local copies, waits for them, and re-layouts  1.28 us (2%)
    pallas_call x1, Pallas kernels, local(): pl.pallas_call(functools.partial(kernel, scale), out_shape=jax.ShapeDtype...  83.2 us

profile of v2, /device:TPU:0, one launch (start us, length us, event | category | flops | bytes accessed | tf_op | source)
XLA Modules:
  0.0 84.5 jit_solution(8574069070172206293)
XLA Ops:
  0.0 83.2 %shard_map.100 = bf16[2,2,4,128]{3,2,1,0:T(4,128)(2,1)} custom-call(bf16[1024,7168]{1,0:T(8,128)(2,1)} %hidden_hbm.1, bf16[224,576]{1,0:T(8,128)(2,1)} %kv_hbm.1, f32[1,512]{1,0:T(1,128)} %bitcast.5, bf16[2,2,4,128]{3,2,1,0:T(4,128)(2,1)} %nope_ref.1, bf16[2,2,4,64]{3,2,1,0:T(4,128)(2,1)} %rope_ref.1, bf16[4,128,512]{2,1,0:T(8,128)(2,1)} %key_up_ref.1, ...), custom_call_target="tpu_custom_call" | custom-call | tf_op jit(solution)/shard_map/pallas_call | solution.py:603
  83.3 1.3 %copy.12 = bf16[2,2,4,128]{3,2,1,0:T(4,128)(2,1)} copy(bf16[2,2,4,128]{3,2,1,0:T(4,128)(2,1)} %shard_map.100) | data formatting | bytes 8192

commit v3 on v2

--- a/solution.py
+++ b/solution.py
@@ -15,13 +15,16 @@
 TAIL = 640
 MESH = pl.DeviceIdType.MESH
 TURNS = (2, 1, 3, 0)
-ONWARD = (0, 1)
+NEAR, SIDE, FAR = 1, 3, 2
+RING = (0, NEAR, SIDE, FAR)
 PLAN = (
-    ("q", 0), ("q", 1), ("p", 0, 0), ("p", 1, 0), ("p", 0, 1), ("p", 0, 2), ("o", 0), ("o", 1), ("q", 2),
-    ("n", 1, 0), ("p", 1, 1), ("n", 0, 0), ("p", 1, 2), ("c",), ("p", 0, 3), ("n", 1, 2), ("n", 1, 1), ("n",
-    0, 1), ("n", 0, 2), ("p", 1, 3), ("n", 0, 3), ("k", 0), ("m", 0, 0), ("m", 0, 1), ("m", 0, 2), ("m", 2,
-    0), ("m", 2, 1), ("n", 1, 3), ("m", 0, 3), ("k", 1), ("m", 2, 2), ("m", 2, 3), ("m", 1, 0), ("m", 1, 1),
-    ("m", 1, 2), ("m", 1, 3), ("m", 3, 0), ("m", 3, 1), ("m", 3, 2), ("m", 3, 3),
+    ("c",), ("q", 0), ("q", 1), ("p", 0, 0), ("p", 1, 0), ("p", 1, 2), ("o", 0), ("q", 2), ("p", 0, 1), ("w",
+    0, 0), ("p", 0, 2), ("k", 0), ("o", 1), ("p", 1, 1), ("m", 0, 0, 0), ("n", 1, 2), ("w", 2, 0), ("m", 0, 0,
+    1), ("n", 1, 0), ("p", 0, 3), ("k", 1), ("m", 2, 0, 0), ("m", 2, 0, 1), ("w", 1, 0), ("p", 1, 3), ("n", 0,
+    0), ("n", 0, 3), ("m", 1, 0, 0), ("w", 0, 1), ("m", 1, 0, 1), ("n", 0, 1), ("n", 0, 2), ("n", 1, 1), ("w",
+    2, 1), ("m", 0, 1, 0), ("n", 1, 3), ("m", 2, 1, 0), ("m", 0, 1, 1), ("m", 2, 1, 1), ("w", 3, 0), ("w", 1,
+    1), ("w", 3, 1), ("m", 3, 0, 0), ("m", 1, 1, 0), ("m", 3, 0, 1), ("m", 1, 1, 1), ("m", 3, 1, 0), ("m", 3,
+    1, 1),
 )
 
 
@@ -33,6 +36,15 @@
 
 def ctx_of(z, y, core):
     return (z * 4 + y) * 2 + core
+
+
+def flip(place_at, turn):
+    low = place_at % 2
+    if turn == 0:
+        return place_at
+    if turn == FAR:
+        return (place_at + 2) % 4
+    return (place_at + (1 - 2 * low if turn == NEAR else 2 * low + 3)) % 4
 
 
 def remote(src, dst, send_sem, recv_sem, device):
@@ -168,7 +180,7 @@
         ):
             pl.semaphore_signal(barrier, inc=1, device_id=device, device_id_type=MESH)
 
-    line = [z, (z + 3) % 4, (z + 1) % 4, (z + 2) % 4]
+    line = [flip(z, turn) for turn in RING]
     own_rows = pl.ds(pl.multiple_of(ctx_of(z, y, core) * depth, 16), depth)
     own_load = pltpu.make_async_copy(kv_hbm, weights.at[own_rows, :], load_sem.at[4])
     own_load.start()
@@ -232,14 +244,14 @@
 
     def places(part):
         first, second = mine[part]
-        along = [first, (first + 3) % 4, (first + 1) % 4, (first + 2) % 4]
+        along = [flip(first, turn) for turn in RING]
         found = {15: (first, second)}
         for index in range(4):
             if index < 3:
                 found[index] = (along[index + 1], second)
-            found[3 + index] = (along[index], (second + 3) % 4)
-            found[7 + index] = (along[index], (second + 1) % 4)
-            found[11 + index] = (along[index], (second + 2) % 4)
+            found[3 + index] = (along[index], flip(second, NEAR))
+            found[7 + index] = (along[index], flip(second, SIDE))
+            found[11 + index] = (along[index], flip(second, FAR))
         return found
 
     table = [places(0), places(1)]
@@ -263,20 +275,21 @@
         first, second = mine[part]
         where = table[part][(15, 0, 1, 2)[index]]
         need(part, (15, 0, 1, 2)[index])
-        send(part, 3 + index, where, (first, (second + 1) % 4))
-        send(part, 7 + index, where, (first, (second + 3) % 4))
+        send(part, 3 + index, where, (first, flip(second, NEAR)))
+        send(part, 7 + index, where, (first, flip(second, SIDE)))
 
     def opposite(part):
         first, second = mine[part]
-        turn = 1 - 2 * core
         need(part, 0, 1)
-        send(part, 2, ((first - turn + 4) % 4, second), ((first + turn + 4) % 4, second))
+        source = jnp.where(core == 0, flip(first, NEAR), flip(first, SIDE))
+        target = jnp.where(core == 0, flip(first, SIDE), flip(first, NEAR))
+        send(part, 2, (source, second), (target, second))
 
     def onward(part, index):
         first, second = mine[part]
-        slot, step = (3 + index, 1) if index in ONWARD else (7 + index, 3)
+        slot, turn = (3 + index, SIDE) if index < 2 else (7 + index, NEAR)
         need(part, slot)
-        send(part, 11 + index, table[part][slot], (first, (second + step) % 4))
+        send(part, 11 + index, table[part][slot], (first, flip(second, turn)))
 
     one_at, two_at = jnp.where(core == 0, z, y), jnp.where(core == 0, y, z)
 
@@ -316,25 +329,35 @@
             for copy in q_copies(stage, step, True):
                 begin(copy)
 
-    def multiply(index, tile):
+    loaded = set()
+
+    def pieces_of(index, side):
+        lines = (15, 0, 1, 2)
+        base = (None, 3, 7, 11)[index]
+        one = [lines[k] if index == 0 else base + k for k in ((0, 1), (2, 3))[side]]
+        two = ((lines[index], 3 + index), (7 + index, 11 + index))[side]
+        return [(0, slot) for slot in one] + [(1, slot) for slot in two]
+
+    def gather(index, side):
+        for part, slot in pieces_of(index, side):
+            need(part, slot)
+
+    def multiply(index, side, tile):
         if tile == 0:
-            slots = (
-                (0, ((15, 0, 1, 2), (3, 4, 5, 6), (7, 8, 9, 10), (11, 12, 13, 14))[index]),
-                (1, ((15, 0, 1, 2)[index], 3 + index, 7 + index, 11 + index)),
-            )
-            for part, group in slots:
-                need(part, *group)
-            for part, group in slots:
-                for slot in group:
-                    pair(part, slot, table[part][slot], 1 - core).wait_recv()
-            loads[index].wait()
-        columns = pl.ds(pl.multiple_of(line[index] * chunk, 128), chunk)
-        down = pl.ds(pl.multiple_of(line[index] * chunk, 16), chunk)
-        span = pl.ds(tile * 256, 256)
+            gather(index, side)
+            for part, slot in pieces_of(index, side):
+                pair(part, slot, table[part][slot], 1 - core).wait_recv()
+            if index not in loaded:
+                loaded.add(index)
+                loads[index].wait()
+        start = line[index] * chunk + (y // 2 if side == 0 else 1 - y // 2) * (chunk // 2)
+        columns = pl.ds(pl.multiple_of(start, 128), chunk // 2)
+        down = pl.ds(pl.multiple_of(start, 128), chunk // 2)
+        span = pl.ds(tile * 512, 512)
         product = jnp.dot(
             hidden[span, columns], weights[down, :], preferred_element_type=jnp.float32
         )
-        if index == 0:
+        if index == 0 and side == 0:
             total[span, :] = product
         else:
             total[span, :] += product
@@ -368,8 +391,8 @@
 
     for part in (0, 1):
         first, second_at = mine[part]
-        send(part, 0, (first, second_at), ((first + 1) % 4, second_at))
-        send(part, 1, (first, second_at), ((first + 3) % 4, second_at))
+        send(part, 0, (first, second_at), (flip(first, NEAR), second_at))
+        send(part, 1, (first, second_at), (flip(first, SIDE), second_at))
     for copy in others:
         copy.start()
     for load in loads:
@@ -386,6 +409,8 @@
             onward(*numbers)
         elif kind == "q":
             q_stage(*numbers)
+        elif kind == "w":
+            gather(*numbers)
         elif kind == "c":
             begin(cache_pair(core))
         elif kind == "k":

time: 84.7 us -> 77.7 us (0.917)
  Pallas kernels: 83.2 us -> 76.2 us
    pallas_call x1, Pallas kernels: 83.2 us -> 76.2 us  [local(): pl.pallas_call(functools.partial(kernel, scale), out_shape=jax.ShapeDtype...]
where the time goes in v3:
time: 77.7 us; the launch traced here: 77.5 us
  Pallas kernels  76.2 us (98%)
  local copies, waits for them, and re-layouts  1.28 us (2%)
    pallas_call x1, Pallas kernels, local(): pl.pallas_call(functools.partial(kernel, scale), out_shape=jax.ShapeDtype...  76.2 us

profile of v3, /device:TPU:0, one launch (start us, length us, event | category | flops | bytes accessed | tf_op | source)
XLA Modules:
  0.0 77.5 jit_solution(7898251430327712553)
XLA Ops:
  0.0 76.2 %shard_map.100 = bf16[2,2,4,128]{3,2,1,0:T(4,128)(2,1)} custom-call(bf16[1024,7168]{1,0:T(8,128)(2,1)} %hidden_hbm.1, bf16[224,576]{1,0:T(8,128)(2,1)} %kv_hbm.1, f32[1,512]{1,0:T(1,128)} %bitcast.5, bf16[2,2,4,128]{3,2,1,0:T(4,128)(2,1)} %nope_ref.1, bf16[2,2,4,64]{3,2,1,0:T(4,128)(2,1)} %rope_ref.1, bf16[4,128,512]{2,1,0:T(8,128)(2,1)} %key_up_ref.1, ...), custom_call_target="tpu_custom_call" | custom-call | tf_op jit(solution)/shard_map/pallas_call | solution.py:628
  76.2 1.3 %copy.12 = bf16[2,2,4,128]{3,2,1,0:T(4,128)(2,1)} copy(bf16[2,2,4,128]{3,2,1,0:T(4,128)(2,1)} %shard_map.100) | data formatting | bytes 8192

commit v4 on v3

--- a/solution.py
+++ b/solution.py
@@ -77,10 +77,12 @@
     best = functools.reduce(jnp.maximum, marks)
     weights = [jnp.exp2(mark - best) for mark in marks]
     amount = functools.reduce(jnp.add, weights)
+    inverse = 1.0 / amount
     block = functools.reduce(
-        jnp.add, [part[..., :LATENT].astype(jnp.float32) * w for part, w in zip(parts, weights)]
+        jnp.add,
+        [part[..., :LATENT].astype(jnp.float32) * (w * inverse) for part, w in zip(parts, weights)],
     )
-    return block / amount, jnp.maximum(best + jnp.log2(amount), LOW)
+    return block, jnp.maximum(best + jnp.log2(amount), LOW)
 
 
 def attend(queries, blocks, scale):
@@ -461,27 +463,28 @@
         some = amount > 0.0
         amount = jnp.where(some, amount, 1.0)
         mark = jnp.where(some, best + jnp.log2(amount), LOW)
-        block, tail = pack(summed / amount, mark)
+        block, tail = pack(summed * (1.0 / amount), mark)
         outgoing[step, :, :, :, :LATENT] = block.reshape(4, 4, 16, LATENT)
         outgoing[step, :, :, :, LATENT:] = tail.reshape(4, 4, 16, TAIL - LATENT)
-        if turn != 0:
-
-            @pl.when(core == 0)
-            def _():
-                out_x(step).start()
+
+        @pl.when(core == 0)
+        def _():
+            for turn in (2, 1, 3):
+                out_y(step, turn).start()
 
         @pl.when(core == 1)
         def _():
             for turn in (2, 1, 3):
                 out_z(step, turn).start()
 
-    def out_x(step):
+    def out_y(step, turn):
+        there = (y + turn) % 4
         return remote(
-            outgoing.at[step],
-            arrived.at[step],
-            one_send.at[step, 0],
-            one_recv.at[step, 0],
-            {"role": (x + TURNS[step]) % 4},
+            outgoing.at[step, :, there],
+            arrived.at[step, turn],
+            one_send.at[step, turn],
+            one_recv.at[step, turn],
+            {"ctx": ctx_of(z, there, core)},
         )
 
     def out_z(step, turn):
@@ -494,16 +497,6 @@
             {"ctx": ctx_of(there, y, core)},
         )
 
-    def next_y(turn):
-        there = (y + turn) % 4
-        return remote(
-            second.at[:, there],
-            second_in.at[turn],
-            two_send.at[turn],
-            two_recv.at[turn],
-            {"ctx": ctx_of(z, there, core)},
-        )
-
     def next_x(step):
         return remote(
             second.at[step],
@@ -539,13 +532,20 @@
         ref[..., LATENT:] = tail
 
     def merge(step):
+        @pl.when(core == 0)
+        def _():
+            for turn in (1, 3, 2):
+                out_y(step, turn).wait_recv()
+
         @pl.when(core == 1)
         def _():
-            for turn in (1, 2, 3):
+            for turn in (1, 3, 2):
                 out_z(step, turn).wait_recv()
-            put(second.at[step], [outgoing[step, z]] + [arrived[step, turn] for turn in (1, 2, 3)])
-            if TURNS[step] != 0:
-                next_x(step).start()
+
+        own = jnp.where(core == 0, outgoing[step, :, y], outgoing[step, z])
+        put(second.at[step], [own] + [arrived[step, turn] for turn in (1, 2, 3)])
+        if TURNS[step] != 0:
+            next_x(step).start()
 
     for step in range(4):
         compute(step)
@@ -563,40 +563,39 @@
             out_ref[index // 2, index % 2] = result[index * 4 : index * 4 + 4].astype(jnp.bfloat16)
 
     others[2].wait()
+    for step in range(3):
+        next_x(step).wait_recv()
+    put(third, [second[3]] + [second_in[step] for step in range(3)])
 
     @pl.when(core == 0)
     def _():
-        for step in range(3):
-            out_x(step).wait_recv()
-        put(second, [outgoing[3]] + [arrived[step] for step in range(3)])
-        for turn in (2, 1, 3):
-            next_y(turn).start()
-        for turn in (1, 3, 2):
-            next_y(turn).wait_recv()
-        put(third, [second[:, y]] + [second_in[turn] for turn in (1, 2, 3)])
         for turn in (2, 1, 3):
             end_z(turn).start()
         for turn in (1, 3, 2):
             end_z(turn).wait_recv()
-        conclude(joined([third[z]] + [third_in[turn] for turn in (1, 2, 3)])[0])
-        for step in range(3):
-            out_x(step).wait_send()
-        for turn in (1, 2, 3):
-            next_y(turn).wait_send()
-            end_z(turn).wait_send()
 
     @pl.when(core == 1)
     def _():
-        for step in range(3):
-            next_x(step).wait_recv()
-        put(third, [second[3]] + [second_in[step] for step in range(3)])
         for turn in (2, 1, 3):
             end_y(turn).start()
         for turn in (1, 3, 2):
             end_y(turn).wait_recv()
-        conclude(joined([third[y]] + [third_in[turn] for turn in (1, 2, 3)])[0])
-        for step in range(3):
-            next_x(step).wait_send()
+
+    own = jnp.where(core == 0, third[z], third[y])
+    conclude(joined([own] + [third_in[turn] for turn in (1, 2, 3)])[0])
+
+    for step in range(3):
+        next_x(step).wait_send()
+
+    @pl.when(core == 0)
+    def _():
+        for turn in (1, 2, 3):
+            for step in range(4):
+                out_y(step, turn).wait_send()
+            end_z(turn).wait_send()
+
+    @pl.when(core == 1)
+    def _():
         for turn in (1, 2, 3):
             for step in range(4):
                 out_z(step, turn).wait_send()

time: 77.7 us -> 74.9 us (0.964)
  Pallas kernels: 76.2 us -> 73.5 us
    pallas_call x1, Pallas kernels: 76.2 us -> 73.5 us  [local(): pl.pallas_call(functools.partial(kernel, scale), out_shape=jax.ShapeDtype...]
where the time goes in v4:
time: 74.9 us; the launch traced here: 74.8 us
  Pallas kernels  73.5 us (98%)
  local copies, waits for them, and re-layouts  1.28 us (2%)
    pallas_call x1, Pallas kernels, local(): pl.pallas_call(functools.partial(kernel, scale), out_shape=jax.ShapeDtype...  73.5 us

profile of v4, /device:TPU:0, one launch (start us, length us, event | category | flops | bytes accessed | tf_op | source)
XLA Modules:
  0.0 74.8 jit_solution(1870282103654697505)
XLA Ops:
  0.0 73.5 %shard_map.100 = bf16[2,2,4,128]{3,2,1,0:T(4,128)(2,1)} custom-call(bf16[1024,7168]{1,0:T(8,128)(2,1)} %hidden_hbm.1, bf16[224,576]{1,0:T(8,128)(2,1)} %kv_hbm.1, f32[1,512]{1,0:T(1,128)} %bitcast.5, bf16[2,2,4,128]{3,2,1,0:T(4,128)(2,1)} %nope_ref.1, bf16[2,2,4,64]{3,2,1,0:T(4,128)(2,1)} %rope_ref.1, bf16[4,128,512]{2,1,0:T(8,128)(2,1)} %key_up_ref.1, ...), custom_call_target="tpu_custom_call" | custom-call | tf_op jit(solution)/shard_map/pallas_call | solution.py:627
  73.5 1.3 %copy.12 = bf16[2,2,4,128]{3,2,1,0:T(4,128)(2,1)} copy(bf16[2,2,4,128]{3,2,1,0:T(4,128)(2,1)} %shard_map.100) | data formatting | bytes 8192

commit v5 on v4

--- a/solution.py
+++ b/solution.py
@@ -124,7 +124,7 @@
     gain_ref,
     nope_ref,
     rope_ref,
-    key_up_ref,
+    key_up_hbm,
     value_up_hbm,
     cache_hbm,
     length_ref,
@@ -137,6 +137,7 @@
     queries,
     cache,
     value_up,
+    key_up,
     pages,
     owner,
     old_best,
@@ -201,23 +202,12 @@
         ),
         pltpu.make_async_copy(cache_hbm, cache.at[core], load_sem.at[6]),
         pltpu.make_async_copy(value_up_hbm, value_up, load_sem.at[7]),
+        pltpu.make_async_copy(key_up_hbm, key_up, load_sem.at[8]),
     ]
 
-    heads = key_up_ref.shape[0]
+    heads = key_up.shape[0]
     row = lax.broadcasted_iota(jnp.int32, (16, 1), 0) % heads
 
-    nope = jnp.concatenate(
-        [nope_ref[r, t].astype(jnp.float32) for r in (0, 1) for t in (0, 1)], axis=0
-    ).astype(jnp.bfloat16)
-    rope = jnp.concatenate(
-        [rope_ref[r, t].astype(jnp.float32) for r in (0, 1) for t in (0, 1)], axis=0
-    )
-    absorbed = jnp.zeros((16, LATENT), jnp.float32)
-    for head in range(heads):
-        product = jnp.dot(nope, key_up_ref[head], preferred_element_type=jnp.float32)
-        absorbed = jnp.where(row == head, product, absorbed)
-    queries[x, z, y, core, :, :LATENT] = absorbed.astype(jnp.bfloat16)
-    queries[x, z, y, core, :, LATENT:] = rope.astype(jnp.bfloat16)
     own_load.wait()
     pl.semaphore_wait(barrier, 10)
 
@@ -395,12 +385,36 @@
         first, second_at = mine[part]
         send(part, 0, (first, second_at), (flip(first, NEAR), second_at))
         send(part, 1, (first, second_at), (flip(first, SIDE), second_at))
-    for copy in others:
+    for copy in (others[3], others[0], others[1], others[2]):
         copy.start()
     for load in loads:
         load.start()
     for part in (0, 1):
         pass_on(part, 15)
+
+    nope = jnp.concatenate(
+        [nope_ref[r, t].astype(jnp.float32) for r in (0, 1) for t in (0, 1)], axis=0
+    ).astype(jnp.bfloat16)
+    rope = jnp.concatenate(
+        [rope_ref[r, t].astype(jnp.float32) for r in (0, 1) for t in (0, 1)], axis=0
+    )
+    others[3].wait()
+    absorbed = jnp.zeros((16, LATENT), jnp.float32)
+    for head in range(heads):
+        product = jnp.dot(nope, key_up[head], preferred_element_type=jnp.float32)
+        absorbed = jnp.where(row == head, product, absorbed)
+    queries[x, z, y, core, :, :LATENT] = absorbed.astype(jnp.bfloat16)
+    queries[x, z, y, core, :, LATENT:] = rope.astype(jnp.bfloat16)
+    others[0].wait()
+    bins = pages[...]
+    request_of = (bins // 64 * 2 + bins % 2).astype(jnp.float32)
+    count = pages.shape[1] // 2
+    page = lax.broadcasted_iota(jnp.int32, (count, count * PAGE), 0)
+    key = lax.broadcasted_iota(jnp.int32, (count, count * PAGE), 1)
+    spread_out = (key // PAGE == page).astype(jnp.float32).astype(jnp.bfloat16)
+    request_of = jnp.concatenate([request_of[:, :count], request_of[:, count:]], axis=0)
+    wide = jnp.concatenate([request_of] * 4, axis=0).astype(jnp.bfloat16)
+    owner[...] = jnp.dot(wide, spread_out, preferred_element_type=jnp.float32)[0:2, :]
 
     for kind, *numbers in PLAN:
         if kind == "p":
@@ -431,17 +445,6 @@
         rows[core, span, :LATENT] = (latent * inverse * gain_ref[...]).astype(jnp.bfloat16)
         rows[core, span, LATENT:] = total[span, LATENT:].astype(jnp.bfloat16)
         begin(rows_pair(tile, core))
-
-    others[0].wait()
-    bins = pages[...]
-    request_of = (bins // 64 * 2 + bins % 2).astype(jnp.float32)
-    count = pages.shape[1] // 2
-    page = lax.broadcasted_iota(jnp.int32, (count, count * PAGE), 0)
-    key = lax.broadcasted_iota(jnp.int32, (count, count * PAGE), 1)
-    spread_out = (key // PAGE == page).astype(jnp.float32).astype(jnp.bfloat16)
-    request_of = jnp.concatenate([request_of[:, :count], request_of[:, count:]], axis=0)
-    wide = jnp.concatenate([request_of] * 4, axis=0).astype(jnp.bfloat16)
-    owner[...] = jnp.dot(wide, spread_out, preferred_element_type=jnp.float32)[0:2, :]
 
     def compute(step):
         turn = TURNS[step]
@@ -563,6 +566,21 @@
             out_ref[index // 2, index % 2] = result[index * 4 : index * 4 + 4].astype(jnp.bfloat16)
 
     others[2].wait()
+    for copy in sends:
+        copy.wait_send()
+
+    @pl.when(core == 0)
+    def _():
+        for turn in (1, 2, 3):
+            for step in range(4):
+                out_y(step, turn).wait_send()
+
+    @pl.when(core == 1)
+    def _():
+        for turn in (1, 2, 3):
+            for step in range(4):
+                out_z(step, turn).wait_send()
+
     for step in range(3):
         next_x(step).wait_recv()
     put(third, [second[3]] + [second_in[step] for step in range(3)])
@@ -590,19 +608,12 @@
     @pl.when(core == 0)
     def _():
         for turn in (1, 2, 3):
-            for step in range(4):
-                out_y(step, turn).wait_send()
             end_z(turn).wait_send()
 
     @pl.when(core == 1)
     def _():
         for turn in (1, 2, 3):
-            for step in range(4):
-                out_z(step, turn).wait_send()
             end_y(turn).wait_send()
-
-    for copy in sends:
-        copy.wait_send()
 
 
 def local(
@@ -627,7 +638,7 @@
     return pl.pallas_call(
         functools.partial(kernel, scale),
         out_shape=jax.ShapeDtypeStruct(q_nope.shape[:3] + (value_up.shape[2],), bf16),
-        in_specs=[hbm, hbm, vmem, vmem, vmem, vmem, hbm, hbm, smem, hbm],
+        in_specs=[hbm, hbm, vmem, vmem, vmem, hbm, hbm, hbm, smem, hbm],
         out_specs=vmem,
         scratch_shapes=[
             pltpu.VMEM(prefill_hidden.shape, bf16),
@@ -637,6 +648,7 @@
             pltpu.VMEM((4, 4, 4, 2, 16, width), bf16),
             pltpu.VMEM((2,) + flipped.shape, bf16),
             pltpu.VMEM(value_up.shape, bf16),
+            pltpu.VMEM(key_up.shape, bf16),
             pltpu.VMEM((1, 2 * rows // PAGE), jnp.int32),
             pltpu.VMEM((2, rows), f32),
             pltpu.VMEM((256, 1), f32),
@@ -648,7 +660,7 @@
             pltpu.VMEM((4, 4, 16, TAIL), bf16),
             pltpu.VMEM((4, 16, TAIL), bf16),
             pltpu.VMEM((4, 16, TAIL), bf16),
-            dma((8,)),
+            dma((9,)),
             dma((2, 15)),
             dma((2, 15)),
             dma((2, 16)),

time: 74.9 us -> 74.5 us (level)
  no operation moved by 1% of the time
where the time goes in v5:
time: 74.5 us; the launch traced here: 74.3 us
  Pallas kernels  73 us (98%)
  local copies, waits for them, and re-layouts  1.28 us (2%)
    pallas_call x1, Pallas kernels, local(): pl.pallas_call(functools.partial(kernel, scale), out_shape=jax.ShapeDtype...  73 us

profile of v5, /device:TPU:0, one launch (start us, length us, event | category | flops | bytes accessed | tf_op | source)
XLA Modules:
  0.0 74.3 jit_solution(9899210695660572367)
XLA Ops:
  0.0 73.0 %shard_map.100 = bf16[2,2,4,128]{3,2,1,0:T(4,128)(2,1)} custom-call(bf16[1024,7168]{1,0:T(8,128)(2,1)} %hidden_hbm.1, bf16[224,576]{1,0:T(8,128)(2,1)} %kv_hbm.1, f32[1,512]{1,0:T(1,128)} %bitcast.5, bf16[2,2,4,128]{3,2,1,0:T(4,128)(2,1)} %nope_ref.1, bf16[2,2,4,64]{3,2,1,0:T(4,128)(2,1)} %rope_ref.1, bf16[4,128,512]{2,1,0:T(8,128)(2,1)} %key_up_hbm.1, ...), custom_call_target="tpu_custom_call" | custom-call | tf_op jit(solution)/shard_map/pallas_call | solution.py:638
  73.0 1.3 %copy.12 = bf16[2,2,4,128]{3,2,1,0:T(4,128)(2,1)} copy(bf16[2,2,4,128]{3,2,1,0:T(4,128)(2,1)} %shard_map.100) | data formatting | bytes 8192
